TPU v7x, 128 devices: a whole 4x4x4 slice. The times are simulated.
128 devices in a mesh: lat: 8 (over z, x_lo), lon: 16 (over y, x_hi, core).
Axes of the slice: x: 4 (x_hi: 2, x_lo: 2; x = x_hi * 2 + x_lo), y: 4, z: 4, core: 2. Of those that a mesh axis runs over, the one named last changes fastest.
Arguments:
- tokens: bfloat16 [144, 384, 1024], P('lat', 'lon'), may hold values from -6 to 6
- qkv_weight: bfloat16 [1024, 3072], replicated, may hold values from -1 to 1
- out_weight: bfloat16 [1024, 1024], replicated, may hold values from -0.1875 to 0.1875
- merge_weight: bfloat16 [4096, 2048], P(None, 'lon'), may hold values from -0.09375 to 0.09375
- up_weight: bfloat16 [2048, 8192], P(None, 'lon'), may hold values from -0.125 to 0.125
- down_weight: bfloat16 [8192, 2048], P('lon'), may hold values from -0.0625 to 0.0625
Outputs:
- middle_out: bfloat16 [144, 384, 1024], P('lat', 'lon')
- coarse_out: bfloat16 [72, 192, 2048], P('lat', 'lon')
All inputs are finite; a program needn't handle non-finite values.
Results may differ from a plain program's by a relative error of at most 0.013.
Values may be sent and summed in bfloat16 or wider, within the bound.
A program may use at most 128 MiB of HBM per device.

v0:
```python
import jax
import jax.numpy as jnp
from jax import lax
from jax.sharding import PartitionSpec as P

HEADS = 16
WLAT = 6
WLON = 12


def extended(value, sides, width, wrap):
    for axis, dim in sides:
        peers, length = (lax.axis_size(axis), value.shape[dim])
        up = [(i, (i + 1) % peers) for i in range(peers if wrap else peers - 1)]
        down = [(j, i) for i, j in up]
        last = lax.slice_in_dim(value, length - width, length, axis=dim)
        first = lax.slice_in_dim(value, 0, width, axis=dim)
        before = lax.ppermute(last, axis, up)
        after = lax.ppermute(first, axis, down)
        value = jnp.concatenate([before, value, after], axis=dim)
    return value


def normalize(values):
    center = values - jnp.mean(values, axis=-1, keepdims=True)
    spread = jnp.mean(center * center, axis=-1, keepdims=True)
    return center * lax.rsqrt(spread + 1e-05)


def to_windows(grid):
    height, breadth, depth = grid.shape
    shaped = grid.reshape(height // WLAT, WLAT, breadth // WLON, WLON, depth)
    return shaped.transpose(0, 2, 1, 3, 4).reshape(-1, WLAT * WLON, depth)


def from_windows(windows, height, breadth):
    depth = windows.shape[-1]
    shaped = windows.reshape(height // WLAT, breadth // WLON, WLAT, WLON, depth)
    return shaped.transpose(0, 2, 1, 3, 4).reshape(height, breadth, depth)


def attend(query, keys, values, key_valid):
    scale = 1.0 / query.shape[-1] ** 0.5
    scores = jnp.einsum("wqhd,wkhd->whqk", query, keys, preferred_element_type=jnp.float32) * scale
    scores = jnp.where(key_valid[:, None, None, :], scores, jnp.float32(-1e30))
    top = jnp.max(scores, axis=-1, keepdims=True)
    raised = jnp.exp(scores - top)
    weights = (raised / jnp.sum(raised, axis=-1, keepdims=True)).astype(jnp.bfloat16)
    summed = jnp.einsum("whqk,wkhd->wqhd", weights, values, preferred_element_type=jnp.float32)
    return summed.astype(jnp.bfloat16)


def extend(field, rim_lat, rim_lon):
    widened = extended(field, (("lon", 1),), rim_lon, True)
    return extended(widened, (("lat", 0),), rim_lat, False)


def per_device(tokens, qkv_weight, out_weight, merge_weight, up_weight, down_weight):
    rows, columns, width = tokens.shape
    rim_lat = WLAT // 2
    rim_lon = WLON // 2
    head_size = width // HEADS
    tall = rows + 2 * rim_lat
    broad = columns + 2 * rim_lon
    normed = normalize(tokens.astype(jnp.float32)).astype(jnp.bfloat16)
    projected = jnp.dot(normed.reshape(-1, width), qkv_weight, preferred_element_type=jnp.float32)
    projected = projected.astype(jnp.bfloat16).reshape(rows, columns, 3 * width)
    query = jnp.pad(projected[:, :, :width], ((rim_lat, rim_lat), (rim_lon, rim_lon), (0, 0)))
    keyval = extend(projected[:, :, width:], rim_lat, rim_lon)
    position = lax.axis_index("lat") * rows - rim_lat + jnp.arange(tall, dtype=jnp.int32)
    row_valid = (position >= 0) & (position < rows * lax.axis_size("lat"))
    flags = to_windows(jnp.broadcast_to(row_valid[:, None, None], (tall, broad, 1)))[..., 0]
    query_windows = to_windows(query)
    count = query_windows.shape[0]
    query_windows = query_windows.reshape(count, WLAT * WLON, HEADS, head_size)
    pair_windows = to_windows(keyval).reshape(count, WLAT * WLON, 2, HEADS, head_size)
    result = attend(query_windows, pair_windows[:, :, 0], pair_windows[:, :, 1], flags)
    attended = from_windows(result.reshape(count, WLAT * WLON, width), tall, broad)
    attended = attended[rim_lat : rim_lat + rows, rim_lon : rim_lon + columns]
    mixed = jnp.dot(attended.reshape(-1, width), out_weight, preferred_element_type=jnp.float32)
    middle_out = (tokens.reshape(-1, width).astype(jnp.float32) + mixed).astype(jnp.bfloat16)
    middle_out = middle_out.reshape(rows, columns, width)
    patches = middle_out.reshape(rows // 2, 2, columns // 2, 2, width).transpose(0, 2, 1, 3, 4)
    merged = normalize(patches.reshape(-1, 4 * width).astype(jnp.float32)).astype(jnp.bfloat16)
    coarse_own = jnp.dot(
        merged,
        lax.all_gather(merge_weight, "lon", axis=1, tiled=True),
        preferred_element_type=jnp.float32,
    ).astype(jnp.bfloat16)
    coarse_band = None
    coarse_band = lax.all_gather(coarse_own, "lon", axis=0, tiled=True)
    coarse_normed = normalize(coarse_band.astype(jnp.float32)).astype(jnp.bfloat16)
    hidden = jax.nn.gelu(
        jnp.dot(coarse_normed, up_weight, preferred_element_type=jnp.float32), approximate=False
    )
    hidden = hidden.astype(jnp.bfloat16)
    summed = lax.psum_scatter(
        jnp.dot(hidden, down_weight, preferred_element_type=jnp.float32).astype(jnp.bfloat16),
        "lon",
        scatter_dimension=0,
        tiled=True,
    ).astype(jnp.float32)
    coarse_out = (coarse_own.astype(jnp.float32) + summed).astype(jnp.bfloat16)
    return (middle_out, coarse_out.reshape(rows // 2, columns // 2, -1))


def solution(mesh):
    return jax.shard_map(
        per_device,
        mesh=mesh,
        in_specs=(P("lat", "lon", None), P(), P(), P(None, "lon"), P(None, "lon"), P("lon", None)),
        out_specs=(P("lat", "lon", None), P("lat", "lon", None)),
        check_vma=False,
    )
```

profile of v0, /device:TPU:1, one launch (start us, length us, event | category | flops | bytes accessed | tf_op | source)
XLA Modules:
  0.0 407.0 jit_solution(3195003166111584990)
XLA Ops:
  12.3 5.9 %convolution_convert_fusion.1 = bf16[432,3072]{1,0:T(8,128)(2,1)S(1)} fusion(bf16[432,1024]{1,0:T(8,128)(2,1)S(1)} %bitcast.55, bf16[1024,3072]{1,0:T(8,128)(2,1)} %param.7), kind=kOutput, calls=%fused_computation.12 | convolution fusion | flops 2719236096 | bytes 9830400 | tf_op jit(solution)/shard_map/dot_general | solution.py:66
  18.4 4.2 %collective-permute-start = (bf16[18,6,2048]{2,1,0:T(8,128)(2,1)S(1)}, bf16[18,6,2048]{2,1,0:T(8,128)(2,1)S(1)}, u32[]{:S(2)}, u32[]{:S(2)}) collective-permute-start(bf16[18,6,2048]{2,1,0:T(8,128)(2,1)S(1)} %get-tuple-element.6), channel_id=1, source_target_pairs={{0,1},{1,2},{2,3},{3,4},{4,5},{5,6},{6,7},{7,8},{8,9},{9,10},{10,1... | collective-permute-start | bytes 1327112 | tf_op jit(solution)/shard_map/ppermute | solution.py:18
  22.8 20.4 %collective-permute-done = bf16[18,6,2048]{2,1,0:T(8,128)(2,1)S(1)} collective-permute-done((bf16[18,6,2048]{2,1,0:T(8,128)(2,1)S(1)}, bf16[18,6,2048]{2,1,0:T(8,128)(2,1)S(1)}, u32[]{:S(2)}, u32[]{:S(2)}) %collective-permute-start) | collective-permute-done | bytes 442400 | tf_op jit(solution)/shard_map/ppermute | solution.py:18
  43.2 5.7 %collective-permute-done.1 = bf16[18,6,2048]{2,1,0:T(8,128)(2,1)S(1)} collective-permute-done((bf16[18,6,2048]{2,1,0:T(8,128)(2,1)S(1)}, bf16[18,6,2048]{2,1,0:T(8,128)(2,1)S(1)}, u32[]{:S(2)}, u32[]{:S(2)}) %collective-permute-start.1) | collective-permute-done | bytes 442400 | tf_op jit(solution)/shard_map/ppermute | solution.py:19
  57.6 4.4 %reshape.113 = bf16[4,6,3,12,1024]{4,1,0,3,2:T(8,128)(2,1)} reshape(bf16[24,36,1024]{2,0,1:T(8,128)(2,1)} %pad.4.clone) | data formatting | bytes 3538944 | tf_op jit(solution)/shard_map/reshape | solution.py:32
  62.0 4.3 %copy.41 = bf16[4,3,6,12,1024]{4,3,2,1,0:T(8,128)(2,1)} copy(bf16[4,3,6,12,1024]{4,2,0,3,1:T(8,128)(2,1)} %bitcast.48) | data formatting | bytes 3538944 | tf_op jit(solution)/shard_map/transpose | solution.py:33
  66.3 6.0 %reshape_reshape.11 = bf16[12,72,16,64]{3,2,1,0:T(8,128)(2,1)} reshape(bf16[4,3,6,12,1024]{4,3,2,1,0:T(8,128)(2,1)} %copy.41) | data formatting | bytes 3538944 | tf_op jit(solution)/shard_map/reshape;reshape | solution.py:75
  72.5 4.7 %collective-permute-done.3 = bf16[3,36,2048]{2,1,0:T(8,128)(2,1)} collective-permute-done((bf16[3,36,2048]{2,1,0:T(8,128)(2,1)}, bf16[3,36,2048]{2,1,0:T(8,128)(2,1)}, u32[]{:S(2)}, u32[]{:S(2)}) %collective-permute-start.3) | collective-permute-done | bytes 442400 | tf_op jit(solution)/shard_map/ppermute | solution.py:19
  83.9 6.9 %reshape.112 = bf16[4,6,3,12,2048]{4,1,0,3,2:T(8,128)(2,1)} reshape(bf16[24,36,2048]{2,0,1:T(8,128)(2,1)} %copy.37) | data formatting | bytes 7077888 | tf_op jit(solution)/shard_map/reshape | solution.py:32
  90.7 7.4 %copy.38 = bf16[4,3,6,12,2048]{4,3,2,1,0:T(8,128)(2,1)} copy(bf16[4,3,6,12,2048]{4,2,0,3,1:T(8,128)(2,1)} %bitcast.47) | data formatting | bytes 7077888 | tf_op jit(solution)/shard_map/transpose | solution.py:33
  98.2 11.6 %reshape_reshape.10 = bf16[12,72,2,16,64]{4,3,2,1,0:T(8,128)(2,1)} reshape(bf16[4,3,6,12,2048]{4,3,2,1,0:T(8,128)(2,1)} %copy.38) | data formatting | bytes 7077888 | tf_op jit(solution)/shard_map/reshape;reshape | solution.py:76
  109.7 7.9 %fusion.95 = (bf16[12,72,1,16,64]{4,3,2,1,0:T(8,128)(2,1)}, bf16[12,72,1,16,64]{4,3,2,1,0:T(8,128)(2,1)}) fusion(bf16[12,72,2,16,64]{4,3,2,1,0:T(8,128)(2,1)} %reshape_reshape.10), kind=kLoop, calls=%fused_computation.130 | loop fusion | bytes 7077888 | tf_op jit(solution)/shard_map/slice | solution.py:77
  117.7 6.5 %copy.51 = bf16[12,72,1,16,64]{1,4,3,0,2:T(8,128)(2,1)} copy(bf16[12,72,1,16,64]{4,3,2,1,0:T(8,128)(2,1)} %get-tuple-element.3) | data formatting | bytes 3538944
  124.1 6.6 %copy.50 = bf16[12,72,1,16,64]{1,4,3,0,2:T(8,128)(2,1)} copy(bf16[12,72,1,16,64]{4,3,2,1,0:T(8,128)(2,1)} %get-tuple-element.2) | data formatting | bytes 3538944
  130.8 5.0 %fusion.9 = f32[12,16,72,72]{2,3,1,0:T(8,128)S(1)} fusion(bf16[12,72,16,64]{3,2,1,0:T(8,128)(2,1)} %reshape_reshape.11, bf16[12,72,1,16,64]{1,4,3,0,2:T(8,128)(2,1)} %copy.51), kind=kOutput, calls=%fused_computation.18 | convolution fusion | flops 127401984 | bytes 7520256 | tf_op jit(solution)/shard_map/wqhd,wkhd->whqk/dot_general | solution.py:44
  142.3 6.4 %copy.45 = bf16[12,72,16,64]{3,2,1,0:T(8,128)(2,1)} copy(bf16[12,72,16,64]{1,3,2,0:T(8,128)(2,1)} %convert_bitcast_fusion) | data formatting | bytes 3538944 | tf_op jit(solution)/shard_map/convert_element_type | solution.py:50
  148.7 6.2 %reshape_reshape.12 = bf16[4,3,6,12,1024]{4,3,2,1,0:T(8,128)(2,1)} reshape(bf16[12,72,16,64]{3,2,1,0:T(8,128)(2,1)} %copy.45) | data formatting | bytes 3538944 | tf_op jit(solution)/shard_map/reshape;reshape | solution.py:38
  181.7 9.7 %convolution_convert_fusion.2 = bf16[108,2048]{1,0:T(8,128)(2,1)} fusion(bf16[4096,2048]{1,0:T(8,128)(2,1)} %all-gather.4.cloned.1.call-done, f32[108,4096]{1,0:T(8,128)} %reshape.119, f32[108]{0:T(128)S(1)} %rsqrt.29, f32[108]{0:T(128)S(1)} %div.33), kind=kOutput, calls=%fused_computation.42 | convolution fusion | flops 1813487616 | bytes 18989920 | tf_op jit(solution)/shard_map/dot_general | solution.py:85
  191.5 72.5 %all-gather.6.cloned.1.call-done = bf16[16,108,2048]{2,1,0:T(8,128)(2,1)} async-done(((bf16[1,108,2048]{2,1,0:T(8,128)(2,1)}), bf16[16,108,2048]{2,1,0:T(8,128)(2,1)}) %all-gather.6.cloned.1.call-update) | async-done | bytes 7077904 | tf_op jit(solution)/shard_map/all_gather | solution.py:91
  268.2 9.6 %reshape.124 = f32[1728,2048]{1,0:T(8,128)} reshape(bf16[16,108,2048]{2,1,0:T(8,128)(2,1)} %all-gather.6.cloned.1.call-done) | data formatting | bytes 21233664 | tf_op jit(solution)/shard_map/convert_element_type | solution.py:92
  277.8 6.5 %multiply_reduce_fusion = f32[1728]{0:T(1024)S(1)} fusion(f32[1728,2048]{1,0:T(8,128)} %reshape.124, f32[1728]{0:T(1024)S(1)} %reshape.127), kind=kLoop, calls=%fused_computation.2 | loop fusion | flops 10615104 | bytes 14169600 | tf_op jit(solution)/shard_map/reduce_sum | solution.py:26
  284.4 20.1 %convolution_convert_fusion = bf16[1728,2048]{1,0:T(8,128)(2,1)} fusion(bf16[512,2048]{1,0:T(8,128)(2,1)S(1)} %copy-done, bf16[2048,512]{1,0:T(8,128)(2,1)} %param.10, f32[1728,2048]{1,0:T(8,128)} %reshape.124, f32[1728]{0:T(1024)S(1)} %add_rsqrt_fusion.1, f32[1728]{0:T(1024)S(1)} %reshape.127), kind=kOutput, calls=%fused_computation.3 | convolution fusion | flops 7319420928 | bytes 25441792 | tf_op jit(solution)/shard_map/dot_general | solution.py:98
  304.5 80.2 %fusion = bf16[112,2048]{1,0:T(8,128)(2,1)S(1)} fusion(bf16[1728,2048]{1,0:T(8,128)(2,1)} %convolution_convert_fusion), kind=kCustom, calls=%all-reduce-scatter | all-reduce-scatter fusion | flops 3670017 | bytes 7537152
  384.8 5.9 %collective-permute-start.4 = (bf16[60,2048]{1,0:T(8,128)(2,1)S(1)}, bf16[60,2048]{1,0:T(8,128)(2,1)S(1)}, u32[]{:S(2)}, u32[]{:S(2)}) collective-permute-start(bf16[60,2048]{1,0:T(8,128)(2,1)S(1)} %slice.45), channel_id=1, source_target_pairs={{0,1},{1,2},{2,3},{3,4},{4,5},{5,6},{6,7},{7,8},{8,9},{9,10},{10,1... | collective-permute-start | bytes 737288
  (69 shorter events, 67.2 us)
Async XLA Ops:
  7.2 277.2 %copy-start = (bf16[512,2048]{1,0:T(8,128)(2,1)S(1)}, bf16[512,2048]{1,0:T(8,128)(2,1)}, u32[]{:S(2)}) copy-start(bf16[512,2048]{1,0:T(8,128)(2,1)} %param.11) | copy-start | bytes 6291460
  7.2 174.5 %all-gather.4.cloned.1.call-start = ((), (), s32[]{:S(2)}) async-start(), calls=%async_computation | async-start | bytes 17825792 | tf_op jit(solution)/shard_map/all_gather | solution.py:87
  7.9 256.0 %all-gather.6.cloned.1.call-start = ((), (), s32[]{:S(2)}) async-start(), calls=%async_computation.1 | async-start | bytes 7798784 | tf_op jit(solution)/shard_map/all_gather | solution.py:91
  18.4 24.8 %collective-permute-start = (bf16[18,6,2048]{2,1,0:T(8,128)(2,1)S(1)}, bf16[18,6,2048]{2,1,0:T(8,128)(2,1)S(1)}, u32[]{:S(2)}, u32[]{:S(2)}) collective-permute-start(bf16[18,6,2048]{2,1,0:T(8,128)(2,1)S(1)} %get-tuple-element.6), channel_id=1, source_target_pairs={{0,1},{1,2},{2,3},{3,4},{4,5},{5,6},{6,7},{7,8},{8,9},{9,10},{10,1... | collective-permute-start | bytes 1327112 | tf_op jit(solution)/shard_map/ppermute | solution.py:18
  22.6 26.2 %collective-permute-start.1 = (bf16[18,6,2048]{2,1,0:T(8,128)(2,1)S(1)}, bf16[18,6,2048]{2,1,0:T(8,128)(2,1)S(1)}, u32[]{:S(2)}, u32[]{:S(2)}) collective-permute-start(bf16[18,6,2048]{2,1,0:T(8,128)(2,1)S(1)} %get-tuple-element.7), channel_id=1, source_target_pairs={{1,0},{2,1},{3,2},{4,3},{5,4},{6,5},{7,6},{8,7},{9,8},{10,9},{11,1... | collective-permute-start | bytes 1327112 | tf_op jit(solution)/shard_map/ppermute | solution.py:19
  22.8 33.1 %copy-start.3 = (bf16[18,24,2048]{2,1,0:T(8,128)(2,1)}, bf16[18,24,2048]{2,1,0:T(8,128)(2,1)S(1)}, u32[]{:S(2)}) copy-start(bf16[18,24,2048]{2,1,0:T(8,128)(2,1)S(1)} %slice.39) | copy-start | bytes 5308420
  50.1 22.4 %collective-permute-start.2 = (bf16[3,36,2048]{2,1,0:T(8,128)(2,1)}, bf16[3,36,2048]{2,1,0:T(8,128)(2,1)}, u32[]{:S(2)}, u32[]{:S(2)}) collective-permute-start(bf16[3,36,2048]{2,1,0:T(8,128)(2,1)} %get-tuple-element.4), channel_id=1, source_target_pairs={{0,16},{16,32},{32,48},{48,64},{64,80},{80,96},{96,112},{1,17},{17... | collective-permute-start | bytes 1327112 | tf_op jit(solution)/shard_map/ppermute | solution.py:18
  54.0 23.2 %collective-permute-start.3 = (bf16[3,36,2048]{2,1,0:T(8,128)(2,1)}, bf16[3,36,2048]{2,1,0:T(8,128)(2,1)}, u32[]{:S(2)}, u32[]{:S(2)}) collective-permute-start(bf16[3,36,2048]{2,1,0:T(8,128)(2,1)} %get-tuple-element.5), channel_id=1, source_target_pairs={{16,0},{32,16},{48,32},{64,48},{80,64},{96,80},{112,96},{17,1},{33... | collective-permute-start | bytes 1327112 | tf_op jit(solution)/shard_map/ppermute | solution.py:19
  135.8 3.7 copy-start.6
  158.9 6.4 %copy-start.4 = (bf16[18,24,1024]{2,1,0:T(8,128)(2,1)S(1)}, bf16[18,24,1024]{2,1,0:T(8,128)(2,1)}, u32[]{:S(2)}) copy-start(bf16[18,24,1024]{2,1,0:T(8,128)(2,1)} %param.6) | copy-start | bytes 2654212
  162.9 2.4 copy-start.8
  170.5 4.0 copy-start.2
  304.5 86.2 %copy-start.7 = (u32[128]{0:T(128)S(1)}, u32[128]{0:T(128)}, u32[]{:S(2)}) copy-start(u32[128]{0:T(128)} %constant.108) | copy-start | bytes 1540
  304.5 93.4 %copy-start.5 = (bf16[108,2048]{1,0:T(8,128)(2,1)S(1)}, bf16[108,2048]{1,0:T(8,128)(2,1)}, u32[]{:S(2)}) copy-start(bf16[108,2048]{1,0:T(8,128)(2,1)} %convolution_convert_fusion.2) | copy-start | bytes 1327108
  304.5 95.5 %copy-start.1 = (bf16[512,2048]{1,0:T(8,128)(2,1)S(1)}, bf16[512,2048]{1,0:T(8,128)(2,1)}, u32[]{:S(2)}) copy-start(bf16[512,2048]{1,0:T(8,128)(2,1)} %param.11) | copy-start | bytes 6291460
  384.8 9.2 %collective-permute-start.4 = (bf16[60,2048]{1,0:T(8,128)(2,1)S(1)}, bf16[60,2048]{1,0:T(8,128)(2,1)S(1)}, u32[]{:S(2)}, u32[]{:S(2)}) collective-permute-start(bf16[60,2048]{1,0:T(8,128)(2,1)S(1)} %slice.45), channel_id=1, source_target_pairs={{0,1},{1,2},{2,3},{3,4},{4,5},{5,6},{6,7},{7,8},{8,9},{9,10},{10,1... | collective-permute-start | bytes 737288
Sparse Core Ops, SparseCore 0:
  10.4 133.1 all-gather.3
  191.6 72.2 all-gather.5
where the time goes:
time: 415 us; the launch traced here: 407 us
  local copies, waits for them, and re-layouts  117 us (28%)
  waiting for transfers between devices  106 us (26%)
  blocking collectives  80.2 us (19%)
  matrix products  45.6 us (11%)
  other arithmetic  27.3 us (7%)
  starting transfers between devices  15.3 us (4%)
  between operations  15.2 us (4%)
    unnamed x1, blocking collectives  80.2 us
    all_gather x1, waiting for transfers between devices, per_device(): coarse_band = lax.all_gather(coarse_own, 'lon', axis=0, tiled=True)  72.5 us
    ppermute x2, waiting for transfers between devices, extended(): before = lax.ppermute(last, axis, up)  20.4 us
    dot_general x1, matrix products, per_device(): jnp.dot(hidden, down_weight, preferred_element_type=jnp.float32)  20.1 us
    unnamed x24, local copies, waits for them, and re-layouts  18.2 us
    transpose x4, local copies, waits for them, and re-layouts, to_windows(): return shaped.transpose(0, 2, 1, 3, 4).reshape(-1, WLAT * WLON, depth)  11.9 us
    another operation x1, local copies, waits for them, and re-layouts, per_device(): to_windows(keyval).reshape(count, WLAT * WLON, 2, HEADS, head_size)  11.6 us
    reshape x2, local copies, waits for them, and re-layouts, to_windows(): shaped = grid.reshape(height // WLAT, WLAT, breadth // WLON, WLON, depth)  11.2 us
  transfers between devices with their start and end apart: 7, of which 5 were waited for; matrix products, arithmetic and copies ran while one was open for 33% of the time, Pallas kernels for 0%

commit v1 on v0

v1 whole, which is shorter than its diff:
```python
import functools

import jax
import jax.numpy as jnp
import numpy as np
from jax import lax
from jax.experimental import pallas as pl
from jax.experimental.pallas import tpu as pltpu
from jax.sharding import PartitionSpec as P

MESH = pl.DeviceIdType.MESH
BF = jnp.bfloat16
F32 = jnp.float32
NEG = -1e30

ROWS, COLS, D, DC, HEADS = 18, 24, 1024, 2048, 16
CELLS = ROWS * COLS
GROUP = 112
HIGH = (3, 6, 6, 3)
WIDE = (6, 12, 6)
TOP = (0, 3, 9, 15)
LEFT = (0, 6, 18)


def _round(n):
    return -(-n // 16) * 16


PIECE = {}
_at = 0
for _b in range(3):
    for _a in range(4):
        PIECE[_a, _b] = (_at, _round(HIGH[_a] * WIDE[_b]), HIGH[_a] * WIDE[_b])
        _at += PIECE[_a, _b][1]
OWN = _at
HALO_W, HALO_E, HALO_N, HALO_S = 0, 160, 320, 432
HALO_NW, HALO_NE, HALO_SW, HALO_SE = 544, 576, 608, 640
HALO = 672


def _tables():
    order = np.zeros((OWN, CELLS), np.float32)
    for (a, b), (at, _, _) in PIECE.items():
        k = 0
        for i in range(HIGH[a]):
            for j in range(WIDE[b]):
                order[at + k, (TOP[a] + i) * COLS + LEFT[b] + j] = 1
                k += 1
    patch = np.zeros((4 * GROUP, CELLS), np.float32)
    for g in range(4):
        for r in range(ROWS // 2):
            for c in range(COLS // 2):
                cell = (2 * r + g // 2) * COLS + 2 * c + g % 2
                patch[g * GROUP + r * (COLS // 2) + c, cell] = 1
    return order, patch


def _window_parts():
    out = []
    for b in range(3):
        for a in range(4):
            at, rows, valid = PIECE[a, b]
            parts = []
            side = "n" if a == 0 else "s" if a == 3 else ""
            if b == 0:
                off = PIECE[a, 2][0] - PIECE[0, 2][0]
                parts.append((HALO_W + off, PIECE[a, 2][1], PIECE[a, 2][2], ""))
            if b == 2:
                off = PIECE[a, 0][0]
                parts.append((HALO_E + off, PIECE[a, 0][1], PIECE[a, 0][2], ""))
            if a == 0:
                off = HALO_N + (0, 32, 80)[b]
                parts.append((off, PIECE[3, b][1], PIECE[3, b][2], side))
            if a == 3:
                off = HALO_S + (0, 32, 80)[b]
                parts.append((off, PIECE[0, b][1], PIECE[0, b][2], side))
            corner = {(0, 0): HALO_NW, (0, 2): HALO_NE, (3, 0): HALO_SW, (3, 2): HALO_SE}
            if (a, b) in corner:
                parts.append((corner[a, b], 32, 18, side))
            out.append(((at, rows, valid), parts))
    return out


WINDOWS = _window_parts()


def _bias():
    bias = np.full((3, 16, 128), NEG, np.float32)
    for edge in range(3):
        for w, ((_, rows, valid), parts) in enumerate(WINDOWS):
            bias[edge, w, :valid] = 0
            at = rows
            for _, prows, pvalid, side in parts:
                gone = (edge == 1 and side == "n") or (edge == 2 and side == "s")
                if not gone:
                    bias[edge, w, at : at + pvalid] = 0
                at += prows
    return bias


def place():
    lat, lon = lax.axis_index("lat"), lax.axis_index("lon")
    z, xl = lat // 2, lat % 2
    y, xh, c = lon // 4, (lon // 2) % 2, lon % 2
    return lat, lon, z, xl, y, xh, c


def norm_rows(x):
    center = x - jnp.mean(x, axis=-1, keepdims=True)
    spread = jnp.mean(center * center, axis=-1, keepdims=True)
    return center * lax.rsqrt(spread + 1e-5)


def loop(n, body):
    def step(i, carry):
        body(i)
        return carry

    lax.fori_loop(0, n, step, 0)


def cols(i, size, base=0):
    return pl.ds(pl.multiple_of(base + i * size, 128), size)


HALO_SENDS = 12
WSEMS = {}
for _n in (
    ["yq+", "yq-", "yqf+", "yqf-"]
    + [f"yr{s}{i}" for s in "+-" for i in (1, 2, 3)]
    + ["yrf1", "yrf3", "yrf2+", "yrf2-"]
    + [f"x{k}" for k in range(4)]
    + [f"z{k}{s}" for k in range(4) for s in ("+", "-", "f+", "f-")]
):
    WSEMS[_n] = len(WSEMS)


def attention_kernel(
    tok, p1, bias, qkvw, outw, mw, p1t, pg,
    mid_out, merged_out, wg,
    qkvv, outv, p1tv, pgv, normed, xp, halo, qkv, kvh, att, attr, mid, mgd,
    lsem, hs, hr, ws, wr,
):
    lat, lon, z, xl, y, xh, c = place()
    north, south = lat > 0, lat < 7
    west, east = (lon + 15) % 16, (lon + 1) % 16
    yp = (lat, (lon + 4) % 16)
    ym = (lat, (lon + 12) % 16)
    zp = ((lat + 2) % 8, lon)
    zm = ((lat + 6) % 8, lon)
    xpart = (2 * z + 1 - xl, 4 * y + 2 * (1 - xh) + c)

    barrier = pltpu.get_barrier_semaphore()

    def greet(dev):
        pl.semaphore_signal(barrier, inc=1, device_id=dev, device_id_type=MESH)

    for dev in ((lat, west), (lat, east), yp, ym, zp, zm, xpart):
        greet(dev)

    @pl.when(north)
    def _():
        for o in (west, lon, east):
            greet((lat - 1, o))

    @pl.when(south)
    def _():
        for o in (west, lon, east):
            greet((lat + 1, o))

    local = [
        pltpu.make_async_copy(qkvw, qkvv, lsem.at[0]),
        pltpu.make_async_copy(p1t, p1tv, lsem.at[1]),
        pltpu.make_async_copy(outw, outv, lsem.at[2]),
        pltpu.make_async_copy(pg, pgv, lsem.at[3]),
        pltpu.make_async_copy(mw, wg.at[2 * y + xh], lsem.at[4]),
    ]
    for cp in local:
        cp.start()

    count = 7 + jnp.where(north, 3, 0) + jnp.where(south, 3, 0)
    pl.semaphore_wait(barrier, count)

    def block(k, other):
        yy = (y + (0, 3, 1, 2)[k]) % 4
        return 2 * yy + (1 - xh if other else xh)

    def rows_of(quarter, part):
        base = (quarter % 4) * 1024
        if part == 0:
            return pl.ds(pl.multiple_of(base, 512), 1024)
        return pl.ds(pl.multiple_of(base + (part - 1) * 512, 512), 512)

    def wcopy(name, slot, quarter, part, dev, own=False):
        rows = rows_of(quarter, part)
        src = mw.at[rows, :] if own else wg.at[slot, rows, :]
        i = WSEMS[name]
        return pltpu.make_async_remote_copy(
            src_ref=src, dst_ref=wg.at[slot, rows, :], send_sem=ws.at[i], recv_sem=wr.at[i],
            device_id=dev, device_id_type=MESH,
        )

    sends = {}

    def send(name, slot, quarter, part, dev, own=False):
        sends[name] = wcopy(name, slot, quarter, part, dev, own)
        sends[name].start()

    def got(name, slot, quarter, part):
        wcopy(name, slot, quarter, part, yp).wait_recv()

    own = block(0, False)
    send("x0", own, z, 0, xpart, own=True)
    send("yq+", own, z, 0, yp, own=True)
    send("yq-", own, z, 0, ym, own=True)

    def pump_y():
        got("yq+", block(1, False), z, 0)
        send("yqf+", block(1, False), z, 1, yp)
        send("x1", block(1, False), z, 0, xpart)
        got("yq-", block(2, False), z, 0)
        send("yqf-", block(2, False), z, 2, ym)
        send("x2", block(2, False), z, 0, xpart)
        for i in (1, 3, 2):
            send(f"yr+{i}", own, z + i, 0, yp, own=True)
            send(f"yr-{i}", own, z + i, 0, ym, own=True)

    def pump_y2():
        got("yqf+", block(3, False), z, 1)
        got("yqf-", block(3, False), z, 2)
        send("x3", block(3, False), z, 0, xpart)

    def pump_x(k):
        got(f"x{k}", block(k, True), z, 0)
        send(f"z{k}+", block(k, True), z, 0, zp)
        send(f"z{k}-", block(k, True), z, 0, zm)

    def pump_z(k):
        got(f"z{k}+", block(k, True), z + 3, 0)
        send(f"z{k}f+", block(k, True), z + 3, 1, zp)
        got(f"z{k}-", block(k, True), z + 1, 0)
        send(f"z{k}f-", block(k, True), z + 1, 2, zm)

    def pump_r1():
        got("yr+1", block(1, False), z + 1, 0)
        send("yrf1", block(1, False), z + 1, 0, yp)
        got("yr-3", block(2, False), z + 3, 0)
        send("yrf3", block(2, False), z + 3, 0, ym)

    def pump_r2():
        got("yr+2", block(1, False), z + 2, 0)
        send("yrf2+", block(1, False), z + 2, 1, yp)
        got("yr-2", block(2, False), z + 2, 0)
        send("yrf2-", block(2, False), z + 2, 2, ym)

    def norm_block(i):
        r = pl.ds(pl.multiple_of(i * 48, 16), 48)
        normed[r, :] = norm_rows(tok[r, :].astype(F32)).astype(BF)

    loop(9, norm_block)

    def permute(i):
        xp[:, cols(i, 256)] = jnp.dot(
            p1[...], normed[:, cols(i, 256)], preferred_element_type=F32
        ).astype(BF)

    loop(4, permute)

    def hcopy(i, src_at, dst_at, rows, dev):
        return pltpu.make_async_remote_copy(
            src_ref=xp.at[pl.ds(src_at, rows), :], dst_ref=halo.at[pl.ds(dst_at, rows), :],
            send_sem=hs.at[i], recv_sem=hr.at[i], device_id=dev, device_id_type=MESH,
        )

    at = {k: v[0] for k, v in PIECE.items()}
    size = {k: v[1] for k, v in PIECE.items()}
    middle_sends = [
        hcopy(0, 0, HALO_E, 160, (lat, west)),
        hcopy(1, at[0, 2], HALO_W, 160, (lat, east)),
    ]
    north_sends = [
        hcopy(2, at[0, 0], HALO_S, 32, (lat - 1, lon)),
        hcopy(3, at[0, 1], HALO_S + 32, 48, (lat - 1, lon)),
        hcopy(4, at[0, 2], HALO_S + 80, 32, (lat - 1, lon)),
        hcopy(5, at[0, 0], HALO_SE, 32, (lat - 1, west)),
        hcopy(6, at[0, 2], HALO_SW, 32, (lat - 1, east)),
    ]
    south_sends = [
        hcopy(7, at[3, 0], HALO_N, 32, (lat + 1, lon)),
        hcopy(8, at[3, 1], HALO_N + 32, 48, (lat + 1, lon)),
        hcopy(9, at[3, 2], HALO_N + 80, 32, (lat + 1, lon)),
        hcopy(10, at[3, 0], HALO_NE, 32, (lat + 1, west)),
        hcopy(11, at[3, 2], HALO_NW, 32, (lat + 1, east)),
    ]
    for cp in middle_sends:
        cp.start()

    @pl.when(north)
    def _():
        for cp in north_sends:
            cp.start()

    @pl.when(south)
    def _():
        for cp in south_sends:
            cp.start()

    @pl.when(jnp.logical_not(north))
    def _():
        halo[HALO_N : HALO_N + 112, :] = jnp.zeros((112, D), BF)
        halo[HALO_NW : HALO_NW + 64, :] = jnp.zeros((64, D), BF)

    @pl.when(jnp.logical_not(south))
    def _():
        halo[HALO_S : HALO_S + 112, :] = jnp.zeros((112, D), BF)
        halo[HALO_SW : HALO_SW + 64, :] = jnp.zeros((64, D), BF)

    local[0].wait()

    def project(i):
        qkv[:, cols(i, 256)] = jnp.dot(
            xp[...], qkvv[:, cols(i, 256)], preferred_element_type=F32
        ).astype(BF)

    loop(6, project)
    pump_y()
    pump_x(0)
    loop(6, lambda i: project(i + 6))

    for cp in middle_sends:
        cp.wait_recv()

    @pl.when(north)
    def _():
        for cp in south_sends:
            cp.wait_recv()

    @pl.when(south)
    def _():
        for cp in north_sends:
            cp.wait_recv()

    def project_halo(i):
        kvh[:, cols(i, 256)] = jnp.dot(
            halo[...], qkvv[:, cols(i, 256, D)], preferred_element_type=F32
        ).astype(BF)

    loop(8, project_halo)
    pump_y2()
    pump_x(1)
    pump_x(2)
    pump_z(0)

    edge = jnp.where(north, jnp.where(south, 0, 2), 1)
    low = lax.broadcasted_iota(jnp.int32, (1, 128), 1) < 64

    def pair(i):
        head = cols(i, 128)
        head_k, head_v = cols(i, 128, D), cols(i, 128, 2 * D)
        for w, ((start, rows, _), parts) in enumerate(WINDOWS):
            r = slice(start, start + rows)
            q = qkv[r, head] * jnp.asarray(0.125, BF)
            zero = jnp.zeros_like(q)
            q = jnp.concatenate([jnp.where(low, q, zero), jnp.where(low, zero, q)], axis=0)
            ks, vs = [qkv[r, head_k]], [qkv[r, head_v]]
            for off, prows, _, _ in parts:
                ks.append(kvh[off : off + prows, head])
                vs.append(kvh[off : off + prows, head_k])
            k = jnp.concatenate(ks, axis=0) if parts else ks[0]
            v = jnp.concatenate(vs, axis=0) if parts else vs[0]
            m = k.shape[0]
            s = lax.dot_general(q, k, (((1,), (1,)), ((), ())), preferred_element_type=F32)
            s = s + bias[edge, w : w + 1, :m]
            e = jnp.exp(s - jnp.max(s, axis=-1, keepdims=True)).astype(BF)
            ve = jnp.concatenate([v, jnp.ones((m, 128), BF)], axis=1)
            o = jnp.dot(e, ve, preferred_element_type=F32)
            num = jnp.where(low, o[:rows, :128], o[rows:, :128])
            den = jnp.where(low, o[:rows, 128:], o[rows:, 128:])
            att[r, head] = (num / den).astype(BF)

    loop(4, pair)
    pump_x(3)
    pump_r1()
    pump_z(1)
    loop(4, lambda i: pair(i + 4))
    pump_z(2)
    pump_r2()

    local[1].wait()

    def unpermute(i):
        attr[:, cols(i, 256)] = jnp.dot(
            p1tv[...], att[:, cols(i, 256)], preferred_element_type=F32
        ).astype(BF)

    loop(4, unpermute)
    local[2].wait()

    def out_project(i):
        mixed = jnp.dot(attr[...], outv[:, cols(i, 256)], preferred_element_type=F32)
        mid[:, cols(i, 256)] = (tok[:, cols(i, 256)].astype(F32) + mixed).astype(BF)

    loop(4, out_project)
    store_mid = pltpu.make_async_copy(mid, mid_out, lsem.at[5])
    store_mid.start()
    local[3].wait()

    def patch(i):
        g, t = i // 4, i % 4
        mgd[:, cols(i, 256)] = jnp.dot(
            pgv[pl.ds(pl.multiple_of(g * GROUP, 16), GROUP), :], mid[:, cols(t, 256)],
            preferred_element_type=F32,
        ).astype(BF)

    loop(16, patch)

    def merge_norm(i):
        r = pl.ds(pl.multiple_of(i * 16, 16), 16)
        mgd[r, :] = norm_rows(mgd[r, :].astype(F32)).astype(BF)

    loop(GROUP // 16, merge_norm)
    store_mgd = pltpu.make_async_copy(mgd, merged_out, lsem.at[6])
    store_mgd.start()

    pump_z(3)
    got("yr+3", block(1, False), z + 3, 0)
    got("yr-1", block(2, False), z + 1, 0)
    got("yrf1", block(3, False), z + 1, 0)
    got("yrf3", block(3, False), z + 3, 0)
    got("yrf2+", block(3, False), z + 2, 1)
    got("yrf2-", block(3, False), z + 2, 2)
    for k in range(4):
        got(f"z{k}f+", block(k, True), z + 2, 1)
        got(f"z{k}f-", block(k, True), z + 2, 2)
    for name in sends:
        sends[name].wait_send()
    for cp in middle_sends:
        cp.wait_send()

    @pl.when(north)
    def _():
        for cp in north_sends:
            cp.wait_send()

    @pl.when(south)
    def _():
        for cp in south_sends:
            cp.wait_send()

    local[4].wait()
    store_mid.wait()
    store_mgd.wait()


AG = {n: i for i, n in enumerate(["01", "10", "30", "11", "31", "20a", "20b", "21a", "21b"])}


def gelu(x):
    return 0.5 * x * (1.0 + lax.erf(x * np.float32(0.5**0.5)))


def coarse_kernel(
    merged, wg, up, down,
    out,
    xs, wv, up2, down2, cc, theirs, coarse, cn, hid, acc, pt, rb,
    lsem, ss, sr, ags, agr, rss, rsr,
):
    lat, lon, z, xl, y, xh, c = place()
    sibling = (lat, lon + 1 - 2 * c)
    yp = (lat, (lon + 4) % 16)
    ym = (lat, (lon + 12) % 16)
    y2 = (lat, (lon + 8) % 16)
    lat_x, lon_x = 2 * z + 1 - xl, 4 * y + 2 * (1 - xh) + c
    xpart = (lat_x, lon_x)
    xyp = (lat_x, (lon_x + 4) % 16)
    xym = (lat_x, (lon_x + 12) % 16)
    xy2 = (lat_x, (lon_x + 8) % 16)
    barrier = pltpu.get_barrier_semaphore()
    everyone = (sibling, yp, ym, y2, xpart, xyp, xym, xy2)
    for dev in everyone:
        pl.semaphore_signal(barrier, inc=1, device_id=dev, device_id_type=MESH)

    mine = pl.ds(pl.multiple_of(c * GROUP, 16), GROUP)
    half = pl.ds(pl.multiple_of(c * 512, 128), 512)
    local = [
        pltpu.make_async_copy(merged, xs.at[mine, :], lsem.at[0]),
        pltpu.make_async_copy(up, up2.at[:, half], lsem.at[1]),
        pltpu.make_async_copy(down, down2.at[half, :], lsem.at[2]),
    ]
    load_w = [
        pltpu.make_async_copy(wg.at[j], wv.at[:, pl.ds(j * 128, 128)], lsem.at[3 + j])
        for j in range(8)
    ]
    local[0].start()
    for cp in load_w:
        cp.start()
    local[1].start()
    local[2].start()

    def remote(src, dst, s, r, i, dev):
        return pltpu.make_async_remote_copy(
            src_ref=src, dst_ref=dst, send_sem=s.at[i], recv_sem=r.at[i], device_id=dev,
            device_id_type=MESH,
        )

    pl.semaphore_wait(barrier, len(everyone))
    pair = [
        remote(merged, xs.at[mine, :], ss, sr, 0, sibling),
        remote(up, up2.at[:, half], ss, sr, 1, sibling),
        remote(down, down2.at[half, :], ss, sr, 2, sibling),
    ]
    for cp in pair:
        cp.start()
    local[0].wait()
    pair[0].wait_recv()
    for cp in load_w:
        cp.wait()

    def merge(i):
        v = jnp.dot(xs[...], wv[:, cols(i, 256)], preferred_element_type=F32).astype(BF)
        cc[0, :, cols(i, 256)] = v[:GROUP]
        cc[1, :, cols(i, 256)] = v[GROUP:]

    loop(4, merge)
    swap = remote(cc.at[1 - c], theirs, ss, sr, 3, sibling)
    swap.start()
    for j in range(8):
        coarse[:, pl.ds(pl.multiple_of((2 * j + c) * 128, 128), 128)] = cc[c, :, j * 128 : (j + 1) * 128]
    swap.wait_recv()
    for j in range(8):
        coarse[:, pl.ds(pl.multiple_of((2 * j + 1 - c) * 128, 128), 128)] = theirs[:, j * 128 : (j + 1) * 128]

    def coarse_norm(i):
        r = pl.ds(pl.multiple_of(i * 16, 16), 16)
        cn[0, 0, r, :] = norm_rows(coarse[r, :].astype(F32)).astype(BF)

    loop(GROUP // 16, coarse_norm)

    own = cn.at[0, 0]
    other = cn.at[0, 1]
    ag = {
        "01": remote(own, cn.at[0, 1], ags, agr, AG["01"], xpart),
        "30": remote(own, cn.at[3, 0], ags, agr, AG["30"], yp),
        "10": remote(own, cn.at[1, 0], ags, agr, AG["10"], ym),
        "31": remote(other, cn.at[3, 1], ags, agr, AG["31"], yp),
        "11": remote(other, cn.at[1, 1], ags, agr, AG["11"], ym),
    }
    A, B = pl.ds(0, 64), pl.ds(64, 48)
    for f in (0, 1):
        ag[f"2{f}a"] = remote(cn.at[3, f, A, :], cn.at[2, f, A, :], ags, agr, AG[f"2{f}a"], yp)
        ag[f"2{f}b"] = remote(cn.at[1, f, B, :], cn.at[2, f, B, :], ags, agr, AG[f"2{f}b"], ym)
    for n in ("01", "30", "10"):
        ag[n].start()

    def ffn(d, keep):
        def up_step(i):
            x = cn[d].reshape(2 * GROUP, DC)
            h = jnp.dot(x, up2[:, cols(i, 256)], preferred_element_type=F32)
            hid[:, cols(i, 256)] = gelu(h).astype(BF)

        loop(4, up_step)

        def down_step(i):
            t = cols(i, 512)
            v = jnp.dot(hid[...], down2[:, t], preferred_element_type=F32)
            if keep:
                acc[:, t] = v[:GROUP] + coarse[:, t].astype(F32)
            else:
                pt[d, 0, :, t] = v[:GROUP].astype(BF)
            pt[d, 1, :, t] = v[GROUP:].astype(BF)

        loop(4, down_step)

    owners = {1: (yp, xyp), 3: (ym, xym), 2: (y2, xy2), 0: (None, xpart)}
    rs = {}
    for d in range(4):
        for f in (0, 1):
            if (d, f) != (0, 0):
                e = (4 - d) % 4
                rs[d, f] = remote(pt.at[d, f], rb.at[e, f], rss, rsr, 2 * e + f, owners[d][f])

    local[1].wait()
    local[2].wait()
    pair[1].wait_recv()
    pair[2].wait_recv()
    ag["01"].wait_recv()
    ag["31"].start()
    ag["11"].start()
    ffn(0, True)
    rs[0, 1].start()
    ag["30"].wait_recv()
    ag["20a"].start()
    ag["10"].wait_recv()
    ag["20b"].start()
    ag["31"].wait_recv()
    ag["21a"].start()
    ag["11"].wait_recv()
    ag["21b"].start()
    ffn(1, False)
    rs[1, 0].start()
    rs[1, 1].start()
    ffn(3, False)
    rs[3, 0].start()
    rs[3, 1].start()
    for n in ("20a", "20b", "21a", "21b"):
        ag[n].wait_recv()
    ffn(2, False)
    rs[2, 0].start()
    rs[2, 1].start()
    for d, f in ((0, 1), (3, 0), (3, 1), (1, 0), (1, 1), (2, 0), (2, 1)):
        e = (4 - d) % 4
        rs[d, f].wait_recv()

        def add(i, e=e, f=f):
            acc[:, cols(i, 512)] += rb[e, f, :, cols(i, 512)].astype(F32)

        loop(4, add)
    for r in range(9):
        out[r] = acc[12 * r : 12 * r + 12, :].astype(BF)
    for cp in pair:
        cp.wait_send()
    swap.wait_send()
    for cp in ag.values():
        cp.wait_send()
    for cp in rs.values():
        cp.wait_send()


VM = pl.BlockSpec(memory_space=pltpu.VMEM)
ANY = pl.BlockSpec(memory_space=pl.ANY)
DMA = pltpu.SemaphoreType.DMA


def per_device(tokens, qkv_weight, out_weight, merge_weight, up_weight, down_weight):
    order, patch = _tables()
    p1 = jnp.asarray(order, BF)
    p1t = jnp.asarray(order.T, BF)
    pg = jnp.asarray(patch, BF)
    mid, merged, wg = pl.pallas_call(
        attention_kernel,
        name="attention",
        out_shape=(
            jax.ShapeDtypeStruct((CELLS, D), BF),
            jax.ShapeDtypeStruct((GROUP, 4 * D), BF),
            jax.ShapeDtypeStruct((8, 4 * D, 128), BF),
        ),
        in_specs=[VM, VM, VM, ANY, ANY, ANY, ANY, ANY],
        out_specs=(ANY, ANY, ANY),
        scratch_shapes=[
            pltpu.VMEM((D, 3 * D), BF),
            pltpu.VMEM((D, D), BF),
            pltpu.VMEM((CELLS, OWN), BF),
            pltpu.VMEM((4 * GROUP, CELLS), BF),
            pltpu.VMEM((CELLS, D), BF),
            pltpu.VMEM((OWN, D), BF),
            pltpu.VMEM((HALO, D), BF),
            pltpu.VMEM((OWN, 3 * D), BF),
            pltpu.VMEM((HALO, 2 * D), BF),
            pltpu.VMEM((OWN, D), BF),
            pltpu.VMEM((CELLS, D), BF),
            pltpu.VMEM((CELLS, D), BF),
            pltpu.VMEM((GROUP, 4 * D), BF),
            DMA((7,)),
            DMA((HALO_SENDS,)),
            DMA((HALO_SENDS,)),
            DMA((len(WSEMS),)),
            DMA((len(WSEMS),)),
        ],
        compiler_params=pltpu.CompilerParams(
            collective_id=0, has_side_effects=True, vmem_limit_bytes=50 * 2**20
        ),
    )(tokens.reshape(CELLS, D), p1, jnp.asarray(_bias()), qkv_weight, out_weight, merge_weight, p1t, pg)
    coarse_out = pl.pallas_call(
        coarse_kernel,
        name="coarse",
        out_shape=jax.ShapeDtypeStruct((ROWS // 2, COLS // 2, DC), BF),
        in_specs=[ANY, ANY, ANY, ANY],
        out_specs=VM,
        scratch_shapes=[
            pltpu.VMEM((2 * GROUP, 4 * D), BF),
            pltpu.VMEM((4 * D, D), BF),
            pltpu.VMEM((DC, D), BF),
            pltpu.VMEM((D, DC), BF),
            pltpu.VMEM((2, GROUP, D), BF),
            pltpu.VMEM((GROUP, D), BF),
            pltpu.VMEM((GROUP, DC), BF),
            pltpu.VMEM((4, 2, GROUP, DC), BF),
            pltpu.VMEM((2 * GROUP, D), BF),
            pltpu.VMEM((GROUP, DC), F32),
            pltpu.VMEM((4, 2, GROUP, DC), BF),
            pltpu.VMEM((4, 2, GROUP, DC), BF),
            DMA((11,)),
            DMA((4,)),
            DMA((4,)),
            DMA((len(AG),)),
            DMA((len(AG),)),
            DMA((8,)),
            DMA((8,)),
        ],
        compiler_params=pltpu.CompilerParams(
            collective_id=1, has_side_effects=True, vmem_limit_bytes=50 * 2**20
        ),
    )(merged, wg, up_weight, down_weight)
    return mid.reshape(ROWS, COLS, D), coarse_out


def solution(mesh):
    return jax.shard_map(
        per_device,
        mesh=mesh,
        in_specs=(P("lat", "lon", None), P(), P(), P(None, "lon"), P(None, "lon"), P("lon", None)),
        out_specs=(P("lat", "lon", None), P("lat", "lon", None)),
        check_vma=False,
    )
```

time: 415 us -> 166 us (0.40); the launches traced: 407 us -> 166 us
  Pallas kernels: 0 us -> 157 us
  local copies, waits for them, and re-layouts: 117 us -> 7.93 us
  waiting for transfers between devices: 106 us -> 0 us
  blocking collectives: 80.2 us -> 0 us
  matrix products: 45.6 us -> 0 us
  other arithmetic: 27.3 us -> 0 us
  starting transfers between devices: 15.3 us -> 0 us
  between operations: 15.2 us -> 0.68 us
    pallas_call x0 -> x2, Pallas kernels: none -> 157 us  [the longest x1 89.5 us: per_device(): pl.pallas_call(coarse_kernel, name='coarse', out_shape=jax.ShapeDtypeStru...]
    unnamed x1 -> x0, blocking collectives: 80.2 us -> none
    all_gather x2 -> x0, waiting for transfers between devices: 72.5 us -> none  [the longest x1 72.5 us: per_device(): coarse_band = lax.all_gather(coarse_own, 'lon', axis=0, tiled=True)]
    dot_general x6 -> x0, matrix products: 45.6 us -> none  [the longest x1 20.1 us: per_device(): jnp.dot(hidden, down_weight, preferred_element_type=jnp.float32)]
    ppermute x4 -> x0, waiting for transfers between devices: 30.8 us -> none  [the longest x2 20.4 us: extended(): before = lax.ppermute(last, axis, up)]
    convert_element_type x5 -> x0, local copies, waits for them, and re-layouts: 27.1 us -> none  [the longest x3 11.1 us: per_device(): patches.reshape(-1, 4 * width).astype(jnp.float32)]
    another operation x3 -> x0, local copies, waits for them, and re-layouts: 23.8 us -> none  [the longest x1 11.6 us: per_device(): to_windows(keyval).reshape(count, WLAT * WLON, 2, HEADS, head_size)]
    reduce_sum x6 -> x0, other arithmetic: 16.7 us -> none  [the longest x3 10.7 us: normalize(): spread = jnp.mean(center * center, axis=-1, keepdims=True)]
  transfers between devices with their start and end apart: 7 -> 0, of which waited for: 5 -> 0; matrix products, arithmetic and copies ran while one was open for 33% -> 0% of each run, Pallas kernels for 0% -> 0%
where the time goes in v1:
time: 166 us
  Pallas kernels  157 us (95%)
  local copies, waits for them, and re-layouts  7.93 us (5%)
    pallas_call x1, Pallas kernels, per_device(): pl.pallas_call(coarse_kernel, name='coarse', out_shape=jax.ShapeDtypeStru...  89.5 us
    pallas_call x1, Pallas kernels, per_device(): pl.pallas_call(attention_kernel, name='attention', out_shape=(jax.ShapeDt...  67.4 us
    unnamed x16, local copies, waits for them, and re-layouts  7.93 us

profile of v1, /device:TPU:1, one launch (start us, length us, event | category | flops | bytes accessed | tf_op | source)
XLA Modules:
  0.0 165.5 jit_solution(17411933143987063517)
XLA Ops:
  0.6 0.0 copy-start.2
  0.6 1.2 copy-done.2
  1.8 0.0 copy-start.3
  1.8 1.1 copy-done.3
  2.9 0.0 copy-start.4
  2.9 1.0 copy-done.4
  3.9 0.0 copy-start.5
  3.9 1.0 copy-done.5
  4.9 0.0 copy-start.6
  4.9 0.7 copy-done.6
  5.7 0.0 copy-start
  5.7 67.4 %attention.1 = (bf16[432,1024]{1,0:T(8,128)(2,1)S(1)}, bf16[112,4096]{1,0:T(8,128)(2,1)}, bf16[8,4096,128]{2,1,0:T(8,128)(2,1)}) custom-call(bf16[432,1024]{1,0:T(8,128)(2,1)S(1)} %bitcast.3, bf16[576,432]{1,0:T(8,128)(2,1)S(1)} %copy-done.3, f32[3,16,128]{2,1,0:T(8,128)S(1)} %copy-done.6, bf16[1024,3072]{1,0:T(8,128)(2,1)} %qkvw.1, ...), custom_call_target="tpu_custom_call" | custom-call | tf_op jit(solution)/shard_map/attention/pallas_call | solution.py:639
  73.1 0.0 copy-done
  73.1 0.0 copy-start.1
  73.1 1.2 copy-done.1
  74.3 89.5 %coarse.1 = bf16[9,12,2048]{2,1,0:T(8,128)(2,1)S(1)} custom-call(bf16[112,4096]{1,0:T(8,128)(2,1)S(1)} %copy-done.1, bf16[8,4096,128]{2,1,0:T(8,128)(2,1)} %get-tuple-element.7.wg, bf16[2048,512]{1,0:T(8,128)(2,1)S(1)} %copy-done, bf16[512,2048]{1,0:T(8,128)(2,1)} %down.1), custom_call_target="tpu_custom_call" | custom-call | tf_op jit(solution)/shard_map/coarse/pallas_call | solution.py:673
  163.8 0.9 copy.14
  164.7 0.8 copy.15
Async XLA Ops:
  0.6 1.2 copy-start.2
  1.8 1.1 copy-start.3
  2.9 1.1 copy-start.4
  3.9 1.0 copy-start.5
  4.9 0.7 copy-start.6
  5.7 67.4 %copy-start = (bf16[2048,512]{1,0:T(8,128)(2,1)S(1)}, bf16[2048,512]{1,0:T(8,128)(2,1)}, u32[]{:S(2)}) copy-start(bf16[2048,512]{1,0:T(8,128)(2,1)} %up.1) | copy-start | bytes 6291460
  73.1 1.2 copy-start.1

commit v2 on v1

v2 whole, which is shorter than its diff:
```python
import functools

import jax
import jax.numpy as jnp
import numpy as np
from jax import lax
from jax.experimental import pallas as pl
from jax.experimental.pallas import tpu as pltpu
from jax.sharding import PartitionSpec as P

MESH = pl.DeviceIdType.MESH
BF = jnp.bfloat16
F32 = jnp.float32
NEG = -1e30

ROWS, COLS, D, DC, HEADS = 18, 24, 1024, 2048, 16
CELLS = ROWS * COLS
GROUP = 112
HIGH = (3, 6, 6, 3)
WIDE = (6, 12, 6)
TOP = (0, 3, 9, 15)
LEFT = (0, 6, 18)


def _round(n):
    return -(-n // 16) * 16


PIECE = {}
_at = 0
for _b in range(3):
    for _a in range(4):
        PIECE[_a, _b] = (_at, _round(HIGH[_a] * WIDE[_b]), HIGH[_a] * WIDE[_b])
        _at += PIECE[_a, _b][1]
OWN = _at
HALO_W, HALO_E, HALO_N, HALO_S = 0, 160, 320, 432
HALO_NW, HALO_NE, HALO_SW, HALO_SE = 544, 576, 608, 640
HALO = 672


def _tables():
    order = np.zeros((OWN, CELLS), np.float32)
    for (a, b), (at, _, _) in PIECE.items():
        k = 0
        for i in range(HIGH[a]):
            for j in range(WIDE[b]):
                order[at + k, (TOP[a] + i) * COLS + LEFT[b] + j] = 1
                k += 1
    patch = np.zeros((4 * GROUP, CELLS), np.float32)
    for g in range(4):
        for r in range(ROWS // 2):
            for c in range(COLS // 2):
                cell = (2 * r + g // 2) * COLS + 2 * c + g % 2
                patch[g * GROUP + r * (COLS // 2) + c, cell] = 1
    return order, patch


def _window_parts():
    out = []
    for b in range(3):
        for a in range(4):
            at, rows, valid = PIECE[a, b]
            parts = []
            side = "n" if a == 0 else "s" if a == 3 else ""
            if b == 0:
                off = PIECE[a, 2][0] - PIECE[0, 2][0]
                parts.append((HALO_W + off, PIECE[a, 2][1], PIECE[a, 2][2], ""))
            if b == 2:
                off = PIECE[a, 0][0]
                parts.append((HALO_E + off, PIECE[a, 0][1], PIECE[a, 0][2], ""))
            if a == 0:
                off = HALO_N + (0, 32, 80)[b]
                parts.append((off, PIECE[3, b][1], PIECE[3, b][2], side))
            if a == 3:
                off = HALO_S + (0, 32, 80)[b]
                parts.append((off, PIECE[0, b][1], PIECE[0, b][2], side))
            corner = {(0, 0): HALO_NW, (0, 2): HALO_NE, (3, 0): HALO_SW, (3, 2): HALO_SE}
            if (a, b) in corner:
                parts.append((corner[a, b], 32, 18, side))
            out.append(((at, rows, valid), parts))
    return out


WINDOWS = _window_parts()


def _bias():
    bias = np.full((3, 16, 128), NEG, np.float32)
    for edge in range(3):
        for w, ((_, rows, valid), parts) in enumerate(WINDOWS):
            bias[edge, w, :valid] = 0
            at = rows
            for _, prows, pvalid, side in parts:
                gone = (edge == 1 and side == "n") or (edge == 2 and side == "s")
                if not gone:
                    bias[edge, w, at : at + pvalid] = 0
                at += prows
    return bias


def place():
    lat, lon = lax.axis_index("lat"), lax.axis_index("lon")
    z, xl = lat // 2, lat % 2
    y, xh, c = lon // 4, (lon // 2) % 2, lon % 2
    return lat, lon, z, xl, y, xh, c


def norm_rows(x):
    center = x - jnp.mean(x, axis=-1, keepdims=True)
    spread = jnp.mean(center * center, axis=-1, keepdims=True)
    return center * lax.rsqrt(spread + 1e-5)


def loop(n, body):
    def step(i, carry):
        body(i)
        return carry

    lax.fori_loop(0, n, step, 0)


def cols(i, size, base=0):
    return pl.ds(pl.multiple_of(base + i * size, 128), size)


HALO_SENDS = 12
WSEMS = {}
for _n in (
    ["yq+", "yq-", "yqf+", "yqf-"]
    + [f"yr{s}{i}" for s in "+-" for i in (1, 2, 3)]
    + ["yrf1", "yrf3", "yrf2+", "yrf2-"]
    + [f"x{k}" for k in range(6)]
    + [f"z{k}{s}" for k in range(6) for s in ("+", "-", "f+", "f-")]
    + [f"s{k}{i}" for k in (4, 5) for i in range(5)]
    + ["up", "down", "merged", "swap"]
    + ["ag+", "ag-", "ag2+", "ag2-", "rs1", "rs2", "rs3"]
):
    WSEMS[_n] = len(WSEMS)
A_ROWS, B_ROWS = pl.ds(0, 64), pl.ds(64, 48)


def gelu(x):
    return 0.5 * x * (1.0 + lax.erf(x * np.float32(0.5**0.5)))


def kernel(
    tok_in, p1_in, bias, qkvw, outw, mw, p1t_in, pg_in, up, down,
    mid_out, out,
    tok, p1, p1t, pg, qkvv, outv, wv, up4, down4,
    normed, xp, halo, qkv, kvh, mid, mgd,
    xs, cc, theirs, coarse, cn, hid, acc, pt, rb,
    lsem, hs, hr, ws, wr,
):
    lat, lon, z, xl, y, xh, c = place()
    north, south = lat > 0, lat < 7
    west, east = (lon + 15) % 16, (lon + 1) % 16
    yp = (lat, (lon + 4) % 16)
    ym = (lat, (lon + 12) % 16)
    y2 = (lat, (lon + 8) % 16)
    zp = ((lat + 2) % 8, lon)
    zm = ((lat + 6) % 8, lon)
    xpart = (2 * z + 1 - xl, 4 * y + 2 * (1 - xh) + c)
    sibling = (lat, lon + 1 - 2 * c)

    barrier = pltpu.get_barrier_semaphore()

    def greet(dev):
        pl.semaphore_signal(barrier, inc=1, device_id=dev, device_id_type=MESH)

    partners = ((lat, west), (lat, east), yp, ym, y2, zp, zm, xpart, sibling)
    for dev in partners:
        greet(dev)

    @pl.when(north)
    def _():
        for o in (west, lon, east):
            greet((lat - 1, o))

    @pl.when(south)
    def _():
        for o in (west, lon, east):
            greet((lat + 1, o))

    own = 2 * y + xh
    local = [
        pltpu.make_async_copy(tok_in, tok, lsem.at[0]),
        pltpu.make_async_copy(p1_in, p1, lsem.at[1]),
        pltpu.make_async_copy(qkvw, qkvv, lsem.at[2]),
        pltpu.make_async_copy(p1t_in, p1t, lsem.at[3]),
        pltpu.make_async_copy(outw, outv, lsem.at[4]),
        pltpu.make_async_copy(pg_in, pg, lsem.at[5]),
        pltpu.make_async_copy(mw, wv.at[own], lsem.at[6]),
        pltpu.make_async_copy(up, up4.at[0], lsem.at[7]),
        pltpu.make_async_copy(down, down4.at[0], lsem.at[8]),
    ]
    for cp in local:
        cp.start()

    count = len(partners) + jnp.where(north, 3, 0) + jnp.where(south, 3, 0)
    pl.semaphore_wait(barrier, count)

    def block(k, other):
        yy = (y + (0, 3, 1, 2)[k]) % 4
        return 2 * yy + (1 - xh if other else xh)

    def rows_of(size, quarter, part):
        base = (quarter % 4) * size
        if part == 0:
            return pl.ds(pl.multiple_of(base, size), size)
        return pl.ds(pl.multiple_of(base + (part - 1) * (size // 2), size // 2), size // 2)

    sends = {}

    def remote(name, src, dst, dev):
        i = WSEMS[name]
        return pltpu.make_async_remote_copy(
            src_ref=src, dst_ref=dst, send_sem=ws.at[i], recv_sem=wr.at[i],
            device_id=dev, device_id_type=MESH,
        )

    def send(name, src, dst, dev):
        sends[name] = remote(name, src, dst, dev)
        sends[name].start()

    def await_to(name, dst):
        remote(name, dst, dst, yp).wait_recv()

    def near(k, quarter, part):
        return wv.at[block(k, False), rows_of(1024, quarter, part), :]

    def send_own(name, quarter, dev):
        send(name, mw.at[rows_of(1024, quarter, 0), :], near(0, quarter, 0), dev)

    def far(k, quarter, part):
        if k < 4:
            return wv.at[block(k, True), rows_of(1024, quarter, part), :]
        if k == 4:
            return up4.at[2, rows_of(512, quarter, part), :]
        return down4.at[2, rows_of(128, quarter, part), :]

    send("x0", mw.at[rows_of(1024, z, 0), :], near(0, z, 0), xpart)
    send_own("yq+", z, yp)
    send_own("yq-", z, ym)

    def pump_y():
        await_to("yq+", near(1, z, 0))
        send("yqf+", near(1, z, 1), near(1, z, 1), yp)
        send("x1", near(1, z, 0), near(1, z, 0), xpart)
        await_to("yq-", near(2, z, 0))
        send("yqf-", near(2, z, 2), near(2, z, 2), ym)
        send("x2", near(2, z, 0), near(2, z, 0), xpart)
        for i in (1, 3, 2):
            send_own(f"yr+{i}", z + i, yp)
            send_own(f"yr-{i}", z + i, ym)

    def pump_y2():
        await_to("yqf+", near(3, z, 1))
        await_to("yqf-", near(3, z, 2))
        send("x3", near(3, z, 0), near(3, z, 0), xpart)

    def send_ffn():
        send("x4", up.at[rows_of(512, z, 0), :], far(4, z, 0), xpart)
        send("x5", down.at[rows_of(128, z, 0), :], far(5, z, 0), xpart)

    def share(k, i, quarter, part):
        if k >= 4:
            src = far(k, quarter, part)
            to = up4 if k == 4 else down4
            dst = to.at[3, rows_of(512 if k == 4 else 128, quarter, part), :]
            send(f"s{k}{i}", src, dst, sibling)

    def pump_x(k):
        await_to(f"x{k}", far(k, z, 0))
        send(f"z{k}+", far(k, z, 0), far(k, z, 0), zp)
        send(f"z{k}-", far(k, z, 0), far(k, z, 0), zm)
        share(k, 0, z, 0)

    def pump_z(k):
        await_to(f"z{k}+", far(k, z + 3, 0))
        send(f"z{k}f+", far(k, z + 3, 1), far(k, z + 3, 1), zp)
        share(k, 1, z + 3, 0)
        await_to(f"z{k}-", far(k, z + 1, 0))
        send(f"z{k}f-", far(k, z + 1, 2), far(k, z + 1, 2), zm)
        share(k, 2, z + 1, 0)

    def end_z(k):
        await_to(f"z{k}f+", far(k, z + 2, 1))
        share(k, 3, z + 2, 1)
        await_to(f"z{k}f-", far(k, z + 2, 2))
        share(k, 4, z + 2, 2)

    def pump_r1():
        await_to("yr+1", near(1, z + 1, 0))
        send("yrf1", near(1, z + 1, 0), near(1, z + 1, 0), yp)
        await_to("yr-3", near(2, z + 3, 0))
        send("yrf3", near(2, z + 3, 0), near(2, z + 3, 0), ym)

    def pump_r2():
        await_to("yr+2", near(1, z + 2, 0))
        send("yrf2+", near(1, z + 2, 1), near(1, z + 2, 1), yp)
        await_to("yr-2", near(2, z + 2, 0))
        send("yrf2-", near(2, z + 2, 2), near(2, z + 2, 2), ym)

    local[0].wait()

    def norm_block(i):
        r = pl.ds(pl.multiple_of(i * 48, 16), 48)
        normed[r, :] = norm_rows(tok[r, :].astype(F32)).astype(BF)

    loop(9, norm_block)
    local[1].wait()

    def permute(i):
        xp[:, cols(i, 256)] = jnp.dot(
            p1[...], normed[:, cols(i, 256)], preferred_element_type=F32
        ).astype(BF)

    loop(4, permute)

    def hcopy(i, src_at, dst_at, rows, dev):
        return pltpu.make_async_remote_copy(
            src_ref=xp.at[pl.ds(src_at, rows), :], dst_ref=halo.at[pl.ds(dst_at, rows), :],
            send_sem=hs.at[i], recv_sem=hr.at[i], device_id=dev, device_id_type=MESH,
        )

    at = {k: v[0] for k, v in PIECE.items()}
    middle_sends = [
        hcopy(0, 0, HALO_E, 160, (lat, west)),
        hcopy(1, at[0, 2], HALO_W, 160, (lat, east)),
    ]
    north_sends = [
        hcopy(2, at[0, 0], HALO_S, 32, (lat - 1, lon)),
        hcopy(3, at[0, 1], HALO_S + 32, 48, (lat - 1, lon)),
        hcopy(4, at[0, 2], HALO_S + 80, 32, (lat - 1, lon)),
        hcopy(5, at[0, 0], HALO_SE, 32, (lat - 1, west)),
        hcopy(6, at[0, 2], HALO_SW, 32, (lat - 1, east)),
    ]
    south_sends = [
        hcopy(7, at[3, 0], HALO_N, 32, (lat + 1, lon)),
        hcopy(8, at[3, 1], HALO_N + 32, 48, (lat + 1, lon)),
        hcopy(9, at[3, 2], HALO_N + 80, 32, (lat + 1, lon)),
        hcopy(10, at[3, 0], HALO_NE, 32, (lat + 1, west)),
        hcopy(11, at[3, 2], HALO_NW, 32, (lat + 1, east)),
    ]
    for cp in middle_sends:
        cp.start()

    @pl.when(north)
    def _():
        for cp in north_sends:
            cp.start()

    @pl.when(south)
    def _():
        for cp in south_sends:
            cp.start()

    @pl.when(jnp.logical_not(north))
    def _():
        halo[HALO_N : HALO_N + 112, :] = jnp.zeros((112, D), BF)
        halo[HALO_NW : HALO_NW + 64, :] = jnp.zeros((64, D), BF)

    @pl.when(jnp.logical_not(south))
    def _():
        halo[HALO_S : HALO_S + 112, :] = jnp.zeros((112, D), BF)
        halo[HALO_SW : HALO_SW + 64, :] = jnp.zeros((64, D), BF)

    pump_y()
    local[2].wait()

    def project(i):
        qkv[:, cols(i, 256)] = jnp.dot(
            xp[...], qkvv[:, cols(i, 256)], preferred_element_type=F32
        ).astype(BF)

    loop(12, project)
    pump_x(0)
    pump_y2()
    send("up", up, up4.at[1], sibling)
    send("down", down, down4.at[1], sibling)

    for cp in middle_sends:
        cp.wait()

    @pl.when(north)
    def _():
        for cp in south_sends:
            cp.wait_recv()
        for cp in north_sends:
            cp.wait_send()

    @pl.when(south)
    def _():
        for cp in north_sends:
            cp.wait_recv()
        for cp in south_sends:
            cp.wait_send()

    def project_halo(i):
        kvh[:, cols(i, 256)] = jnp.dot(
            halo[...], qkvv[:, cols(i, 256, D)], preferred_element_type=F32
        ).astype(BF)

    loop(8, project_halo)
    pump_x(1)
    pump_x(2)
    pump_z(0)

    edge = jnp.where(north, jnp.where(south, 0, 2), 1)
    low = lax.broadcasted_iota(jnp.int32, (1, 128), 1) < 64
    att = xp

    def pair(i):
        head = cols(i, 128)
        head_k, head_v = cols(i, 128, D), cols(i, 128, 2 * D)
        for w, ((start, rows, _), parts) in enumerate(WINDOWS):
            r = slice(start, start + rows)
            q = qkv[r, head] * jnp.asarray(0.125, BF)
            zero = jnp.zeros_like(q)
            q = jnp.concatenate([jnp.where(low, q, zero), jnp.where(low, zero, q)], axis=0)
            ks, vs = [qkv[r, head_k]], [qkv[r, head_v]]
            for off, prows, _, _ in parts:
                ks.append(kvh[off : off + prows, head])
                vs.append(kvh[off : off + prows, head_k])
            k = jnp.concatenate(ks, axis=0) if parts else ks[0]
            v = jnp.concatenate(vs, axis=0) if parts else vs[0]
            m = k.shape[0]
            s = lax.dot_general(q, k, (((1,), (1,)), ((), ())), preferred_element_type=F32)
            s = s + bias[edge, w : w + 1, :m]
            e = jnp.exp(s - jnp.max(s, axis=-1, keepdims=True)).astype(BF)
            ve = jnp.concatenate([v, jnp.ones((m, 128), BF)], axis=1)
            o = jnp.dot(e, ve, preferred_element_type=F32)
            num = jnp.where(low, o[:rows, :128], o[rows:, :128])
            den = jnp.where(low, o[:rows, 128:], o[rows:, 128:])
            att[r, head] = (num / den).astype(BF)

    def pair_late(i):
        pair(i + 4)

    loop(4, pair)
    pump_x(3)
    pump_r1()
    pump_z(1)
    send_ffn()
    loop(4, pair_late)
    pump_z(2)
    pump_r2()

    local[3].wait()
    attr = normed

    def unpermute(i):
        attr[:, cols(i, 256)] = jnp.dot(
            p1t[...], att[:, cols(i, 256)], preferred_element_type=F32
        ).astype(BF)

    loop(4, unpermute)
    local[4].wait()

    def out_project(i):
        mixed = jnp.dot(attr[...], outv[:, cols(i, 256)], preferred_element_type=F32)
        mid[:, cols(i, 256)] = (tok[:, cols(i, 256)].astype(F32) + mixed).astype(BF)

    loop(4, out_project)
    store_mid = pltpu.make_async_copy(mid, mid_out, lsem.at[9])
    store_mid.start()
    pump_z(3)
    local[5].wait()

    def patch(i):
        g, t = i // 4, i % 4
        mgd[:, cols(i, 256)] = jnp.dot(
            pg[pl.ds(pl.multiple_of(g * GROUP, 16), GROUP), :], mid[:, cols(t, 256)],
            preferred_element_type=F32,
        ).astype(BF)

    loop(16, patch)

    def merge_norm(i):
        r = pl.ds(pl.multiple_of(i * 16, 16), 16)
        mgd[r, :] = norm_rows(mgd[r, :].astype(F32)).astype(BF)

    loop(GROUP // 16, merge_norm)
    mine = pl.ds(pl.multiple_of(c * GROUP, 16), GROUP)
    send("merged", mgd, xs.at[mine, :], sibling)
    keep_mgd = pltpu.make_async_copy(mgd, xs.at[mine, :], lsem.at[10])
    keep_mgd.start()

    local[6].wait()
    await_to("yr+3", near(1, z + 3, 0))
    await_to("yr-1", near(2, z + 1, 0))
    await_to("yrf1", near(3, z + 1, 0))
    await_to("yrf3", near(3, z + 3, 0))
    await_to("yrf2+", near(3, z + 2, 1))
    await_to("yrf2-", near(3, z + 2, 2))
    for k in range(4):
        end_z(k)
    pump_x(4)
    pump_x(5)
    keep_mgd.wait()
    theirs_rows = pl.ds(pl.multiple_of((1 - c) * GROUP, 16), GROUP)
    await_to("merged", xs.at[theirs_rows, :])

    def merge(i):
        v = jnp.zeros((2 * GROUP, 256), F32)
        for g in range(4):
            r = slice(g * D, (g + 1) * D)
            w = jnp.concatenate([wv[2 * i, r, :], wv[2 * i + 1, r, :]], axis=1)
            v += jnp.dot(xs[:, r], w, preferred_element_type=F32)
        v = v.astype(BF)
        cc[0, :, cols(i, 256)] = v[:GROUP]
        cc[1, :, cols(i, 256)] = v[GROUP:]

    loop(4, merge)
    send("swap", cc.at[1 - c], theirs, sibling)
    for j in range(8):
        coarse[:, pl.ds(pl.multiple_of((2 * j + c) * 128, 128), 128)] = cc[c, :, j * 128 : (j + 1) * 128]
    await_to("swap", theirs)
    for j in range(8):
        coarse[:, pl.ds(pl.multiple_of((2 * j + 1 - c) * 128, 128), 128)] = theirs[:, j * 128 : (j + 1) * 128]

    def coarse_norm(i):
        r = pl.ds(pl.multiple_of(i * 16, 16), 16)
        cn[0, r, :] = norm_rows(coarse[r, :].astype(F32)).astype(BF)

    loop(GROUP // 16, coarse_norm)

    send("ag+", cn.at[0], cn.at[2], yp)
    send("ag-", cn.at[0], cn.at[3], ym)
    pump_z(4)
    pump_z(5)
    for n in (7, 8):
        local[n].wait()
    await_to("up", up4.at[1])
    await_to("down", down4.at[1])

    def ffn(first, count):
        rows = count * GROUP

        def up_step(i):
            q, t = i // 2, i % 2
            x = cn[first : first + count].reshape(rows, DC)
            h = jnp.dot(x, up4[q, :, cols(t, 256)], preferred_element_type=F32)
            hid[:rows, cols(i, 256)] = gelu(h).astype(BF)

        loop(8, up_step)

        def down_step(i):
            t = cols(i, 256)
            v = jnp.zeros((rows, 256), F32)
            for q in range(4):
                v += jnp.dot(hid[:rows, q * 512 : (q + 1) * 512], down4[q, :, t], preferred_element_type=F32)
            for n in range(count):
                part = v[n * GROUP : (n + 1) * GROUP]
                if first + n == 0:
                    acc[:, t] = part + coarse[:, t].astype(F32)
                else:
                    pt[first + n, :, t] = part.astype(BF)

        loop(8, down_step)

    await_to("ag+", cn.at[2])
    send("ag2+", cn.at[2, A_ROWS, :], cn.at[1, A_ROWS, :], yp)
    await_to("ag-", cn.at[3])
    send("ag2-", cn.at[3, B_ROWS, :], cn.at[1, B_ROWS, :], ym)
    end_z(4)
    end_z(5)
    for k in (4, 5):
        to, size = (up4, 512) if k == 4 else (down4, 128)
        for i, (quarter, part) in enumerate(((z, 0), (z + 3, 0), (z + 1, 0), (z + 2, 1), (z + 2, 2))):
            await_to(f"s{k}{i}", to.at[3, rows_of(size, quarter, part), :])
    ffn(2, 2)
    send("rs2", pt.at[2], rb.at[3], ym)
    send("rs3", pt.at[3], rb.at[2], yp)
    await_to("ag2+", cn.at[1, A_ROWS, :])
    await_to("ag2-", cn.at[1, B_ROWS, :])
    ffn(0, 2)
    send("rs1", pt.at[1], rb.at[1], y2)
    await_to("rs2", rb.at[3])
    await_to("rs3", rb.at[2])

    def add_near(i):
        t = cols(i, 512)
        acc[:, t] += rb[2, :, t].astype(F32) + rb[3, :, t].astype(F32)

    loop(4, add_near)
    await_to("rs1", rb.at[1])

    def add_far(i):
        t = cols(i, 512)
        acc[:, t] += rb[1, :, t].astype(F32)

    loop(4, add_far)
    for r in range(9):
        out[r] = acc[12 * r : 12 * r + 12, :].astype(BF)
    for cp in sends.values():
        cp.wait_send()
    store_mid.wait()


VM = pl.BlockSpec(memory_space=pltpu.VMEM)
HBM = pl.BlockSpec(memory_space=pltpu.HBM)
DMA = pltpu.SemaphoreType.DMA


def per_device(tokens, qkv_weight, out_weight, merge_weight, up_weight, down_weight):
    order, patch = _tables()
    p1 = jnp.asarray(order, BF)
    p1t = jnp.asarray(order.T, BF)
    pg = jnp.asarray(patch, BF)

    def vmem(*shape, kind=BF):
        return pltpu.VMEM(shape, kind)

    mid, coarse_out = pl.pallas_call(
        kernel,
        name="whole",
        out_shape=(
            jax.ShapeDtypeStruct((CELLS, D), BF),
            jax.ShapeDtypeStruct((ROWS // 2, COLS // 2, DC), BF),
        ),
        in_specs=[HBM, HBM, VM] + [HBM] * 7,
        out_specs=(HBM, VM),
        scratch_shapes=[
            vmem(CELLS, D),
            vmem(OWN, CELLS),
            vmem(CELLS, OWN),
            vmem(4 * GROUP, CELLS),
            vmem(D, 3 * D),
            vmem(D, D),
            vmem(8, 4 * D, 128),
            vmem(4, DC, 512),
            vmem(4, 512, DC),
            vmem(CELLS, D),
            vmem(OWN, D),
            vmem(HALO, D),
            vmem(OWN, 3 * D),
            vmem(HALO, 2 * D),
            vmem(CELLS, D),
            vmem(GROUP, 4 * D),
            vmem(2 * GROUP, 4 * D),
            vmem(2, GROUP, D),
            vmem(GROUP, D),
            vmem(GROUP, DC),
            vmem(4, GROUP, DC),
            vmem(2 * GROUP, DC),
            vmem(GROUP, DC, kind=F32),
            vmem(4, GROUP, DC),
            vmem(4, GROUP, DC),
            DMA((11,)),
            DMA((HALO_SENDS,)),
            DMA((HALO_SENDS,)),
            DMA((len(WSEMS),)),
            DMA((len(WSEMS),)),
        ],
        compiler_params=pltpu.CompilerParams(
            collective_id=0, has_side_effects=True, vmem_limit_bytes=62 * 2**20
        ),
    )(
        tokens.reshape(CELLS, D), p1, jnp.asarray(_bias()), qkv_weight, out_weight, merge_weight, p1t, pg,
        up_weight, down_weight,
    )
    return mid.reshape(ROWS, COLS, D), coarse_out


def solution(mesh):
    return jax.shard_map(
        per_device,
        mesh=mesh,
        in_specs=(P("lat", "lon", None), P(), P(), P(None, "lon"), P(None, "lon"), P("lon", None)),
        out_specs=(P("lat", "lon", None), P("lat", "lon", None)),
        check_vma=False,
    )
```

time: 166 us -> 140 us (0.84)
  Pallas kernels: 157 us -> 136 us
  local copies, waits for them, and re-layouts: 7.93 us -> 3.02 us
    pallas_call x2 -> x1, Pallas kernels: 157 us -> 136 us  [per_device(): pl.pallas_call(kernel, name='whole', out_shape=(jax.ShapeDtypeStruct((CEL...]
    unnamed x16 -> x4, local copies, waits for them, and re-layouts: 7.93 us -> 3.02 us
where the time goes in v2:
time: 140 us
  Pallas kernels  136 us (97%)
  local copies, waits for them, and re-layouts  3.02 us (2%)
    pallas_call x1, Pallas kernels, per_device(): pl.pallas_call(kernel, name='whole', out_shape=(jax.ShapeDtypeStruct((CEL...  136 us
    unnamed x4, local copies, waits for them, and re-layouts  3.02 us

profile of v2, /device:TPU:1, one launch (start us, length us, event | category | flops | bytes accessed | tf_op | source)
XLA Modules:
  0.0 139.7 jit_solution(16372838665999931106)
XLA Ops:
  0.6 136.0 %whole.1 = (bf16[432,1024]{1,0:T(8,128)(2,1)}, bf16[9,12,2048]{2,1,0:T(8,128)(2,1)}) custom-call(bf16[432,1024]{1,0:T(8,128)(2,1)} %bitcast.3, bf16[576,432]{1,0:T(8,128)(2,1)} %constant.8.clone.p1_in, f32[3,16,128]{2,1,0:T(8,128)} %constant.11.clone.bias, bf16[1024,3072]{1,0:T(8,128)(2,1)} %qkvw.1, bf16[1024,1024]{1,0:T(8,128)(2,1)} %outw.1, ...), custom_call_target="tpu_custom_call" | custom-call | tf_op jit(solution)/shard_map/whole/pallas_call | solution.py:615
  136.6 0.0 copy-start
  136.7 2.2 %copy.14 = bf16[18,24,1024]{2,1,0:T(8,128)(2,1)} copy(bf16[18,24,1024]{2,1,0:T(8,128)(2,1)} %bitcast.2) | data formatting | bytes 1769472
  138.9 0.0 copy-done
  138.9 0.8 copy.15
Async XLA Ops:
  136.6 2.2 %copy-start = (bf16[9,12,2048]{2,1,0:T(8,128)(2,1)S(1)}, bf16[9,12,2048]{2,1,0:T(8,128)(2,1)}, u32[]{:S(2)}) copy-start(bf16[9,12,2048]{2,1,0:T(8,128)(2,1)} %get-tuple-element.9) | copy-start | bytes 1327108

commit v3 on v2

--- a/solution.py
+++ b/solution.py
@@ -33,9 +33,10 @@
         PIECE[_a, _b] = (_at, _round(HIGH[_a] * WIDE[_b]), HIGH[_a] * WIDE[_b])
         _at += PIECE[_a, _b][1]
 OWN = _at
-HALO_W, HALO_E, HALO_N, HALO_S = 0, 160, 320, 432
-HALO_NW, HALO_NE, HALO_SW, HALO_SE = 544, 576, 608, 640
-HALO = 672
+SEND_W, SEND_E, SEND_N, SEND_S, SENT = 0, 112, 224, 304, 384
+HALO_W, HALO_E, HALO_N, HALO_S = 0, 112, 224, 304
+HALO_NW, HALO_NE, HALO_SW, HALO_SE = 384, 416, 448, 480
+HALO = 512
 
 
 def _tables():
@@ -46,38 +47,49 @@
             for j in range(WIDE[b]):
                 order[at + k, (TOP[a] + i) * COLS + LEFT[b] + j] = 1
                 k += 1
+    packed = np.zeros((SENT, CELLS), np.float32)
+    column = [(a, 0) for a in range(4)]
+    for start, pieces in (
+        (SEND_W, column),
+        (SEND_E, [(a, 2) for a, _ in column]),
+        (SEND_N, [(0, b) for b in range(3)]),
+        (SEND_S, [(3, b) for b in range(3)]),
+    ):
+        k = start
+        for a, b in pieces:
+            n = PIECE[a, b][2]
+            packed[k : k + n] = order[PIECE[a, b][0] : PIECE[a, b][0] + n]
+            k += n
     patch = np.zeros((4 * GROUP, CELLS), np.float32)
     for g in range(4):
         for r in range(ROWS // 2):
             for c in range(COLS // 2):
                 cell = (2 * r + g // 2) * COLS + 2 * c + g % 2
                 patch[g * GROUP + r * (COLS // 2) + c, cell] = 1
-    return order, patch
+    return order, packed, patch
+
+
+def _span(base, start, count, side):
+    low = start // 16 * 16
+    return base + low, _round(start + count) - low, start - low, start - low + count, side
 
 
 def _window_parts():
     out = []
+    along, across = ((0, 18), (18, 36), (54, 36), (90, 18)), ((0, 18), (18, 36), (54, 18))
     for b in range(3):
         for a in range(4):
-            at, rows, valid = PIECE[a, b]
+            side = "n" if a == 0 else "s" if a == 3 else ""
             parts = []
-            side = "n" if a == 0 else "s" if a == 3 else ""
-            if b == 0:
-                off = PIECE[a, 2][0] - PIECE[0, 2][0]
-                parts.append((HALO_W + off, PIECE[a, 2][1], PIECE[a, 2][2], ""))
-            if b == 2:
-                off = PIECE[a, 0][0]
-                parts.append((HALO_E + off, PIECE[a, 0][1], PIECE[a, 0][2], ""))
-            if a == 0:
-                off = HALO_N + (0, 32, 80)[b]
-                parts.append((off, PIECE[3, b][1], PIECE[3, b][2], side))
-            if a == 3:
-                off = HALO_S + (0, 32, 80)[b]
-                parts.append((off, PIECE[0, b][1], PIECE[0, b][2], side))
+            if b != 1:
+                parts.append(_span(HALO_W if b == 0 else HALO_E, *along[a], ""))
+            if side:
+                parts.append(_span(HALO_N if a == 0 else HALO_S, *across[b], side))
             corner = {(0, 0): HALO_NW, (0, 2): HALO_NE, (3, 0): HALO_SW, (3, 2): HALO_SE}
             if (a, b) in corner:
-                parts.append((corner[a, b], 32, 18, side))
-            out.append(((at, rows, valid), parts))
+                first = 6 if b == 0 else 0
+                parts.append((corner[a, b], 32, first, first + 18, side))
+            out.append((PIECE[a, b], parts))
     return out
 
 
@@ -90,10 +102,10 @@
         for w, ((_, rows, valid), parts) in enumerate(WINDOWS):
             bias[edge, w, :valid] = 0
             at = rows
-            for _, prows, pvalid, side in parts:
+            for _, prows, first, last, side in parts:
                 gone = (edge == 1 and side == "n") or (edge == 2 and side == "s")
                 if not gone:
-                    bias[edge, w, at : at + pvalid] = 0
+                    bias[edge, w, at + first : at + last] = 0
                 at += prows
     return bias
 
@@ -123,7 +135,7 @@
     return pl.ds(pl.multiple_of(base + i * size, 128), size)
 
 
-HALO_SENDS = 12
+HALO_SENDS = 8
 WSEMS = {}
 for _n in (
     ["yq+", "yq-", "yqf+", "yqf-"]
@@ -131,8 +143,9 @@
     + ["yrf1", "yrf3", "yrf2+", "yrf2-"]
     + [f"x{k}" for k in range(6)]
     + [f"z{k}{s}" for k in range(6) for s in ("+", "-", "f+", "f-")]
-    + [f"s{k}{i}" for k in (4, 5) for i in range(5)]
-    + ["up", "down", "merged", "swap"]
+    + [f"n{k}{i}" for k in (4, 5) for i in range(5)]
+    + [f"s{k}{i}" for k in (4, 5) for i in range(2)]
+    + ["up", "down", "merged", "swap0", "swap1"]
     + ["ag+", "ag-", "ag2+", "ag2-", "rs1", "rs2", "rs3"]
 ):
     WSEMS[_n] = len(WSEMS)
@@ -144,10 +157,10 @@
 
 
 def kernel(
-    tok_in, p1_in, bias, qkvw, outw, mw, p1t_in, pg_in, up, down,
+    tok_in, ps_in, p1_in, bias, qkvw, outw, mw, p1t_in, pg_in, up, down,
     mid_out, out,
-    tok, p1, p1t, pg, qkvv, outv, wv, up4, down4,
-    normed, xp, halo, qkv, kvh, mid, mgd,
+    tok, ps, p1, p1t, pg, qkvv, outv, wv, up4, down4,
+    normed, packed, xp, halo, qkv, kvh, mid, mgd,
     xs, cc, theirs, coarse, cn, hid, acc, pt, rb,
     lsem, hs, hr, ws, wr,
 ):
@@ -160,6 +173,7 @@
     zp = ((lat + 2) % 8, lon)
     zm = ((lat + 6) % 8, lon)
     xpart = (2 * z + 1 - xl, 4 * y + 2 * (1 - xh) + c)
+    xn = (lat + 1 - 2 * xl, lon)
     sibling = (lat, lon + 1 - 2 * c)
 
     barrier = pltpu.get_barrier_semaphore()
@@ -167,7 +181,7 @@
     def greet(dev):
         pl.semaphore_signal(barrier, inc=1, device_id=dev, device_id_type=MESH)
 
-    partners = ((lat, west), (lat, east), yp, ym, y2, zp, zm, xpart, sibling)
+    partners = ((lat, west), (lat, east), yp, ym, y2, zp, zm, xpart, xn, sibling)
     for dev in partners:
         greet(dev)
 
@@ -193,8 +207,11 @@
         pltpu.make_async_copy(up, up4.at[0], lsem.at[7]),
         pltpu.make_async_copy(down, down4.at[0], lsem.at[8]),
     ]
-    for cp in local:
-        cp.start()
+    early = pltpu.make_async_copy(ps_in, ps, lsem.at[11])
+    local[0].start()
+    early.start()
+    local[1].start()
+    local[2].start()
 
     count = len(partners) + jnp.where(north, 3, 0) + jnp.where(south, 3, 0)
     pl.semaphore_wait(barrier, count)
@@ -231,16 +248,20 @@
     def send_own(name, quarter, dev):
         send(name, mw.at[rows_of(1024, quarter, 0), :], near(0, quarter, 0), dev)
 
-    def far(k, quarter, part):
+    def far(k, quarter, part, half=xl):
         if k < 4:
             return wv.at[block(k, True), rows_of(1024, quarter, part), :]
-        if k == 4:
-            return up4.at[2, rows_of(512, quarter, part), :]
-        return down4.at[2, rows_of(128, quarter, part), :]
-
-    send("x0", mw.at[rows_of(1024, z, 0), :], near(0, z, 0), xpart)
-    send_own("yq+", z, yp)
-    send_own("yq-", z, ym)
+        size = 256 if k == 4 else 64
+        base = (quarter % 4) * size + half * 4 * size
+        if part == 0:
+            rows = pl.ds(pl.multiple_of(base, size), size)
+        else:
+            rows = pl.ds(pl.multiple_of(base + (part - 1) * (size // 2), size // 2), size // 2)
+        return (up4 if k == 4 else down4).at[2, rows, :]
+
+    def half_rows(k, half):
+        size = 1024 if k == 4 else 256
+        return pl.ds(pl.multiple_of(half * size, size), size)
 
     def pump_y():
         await_to("yq+", near(1, z, 0))
@@ -259,35 +280,43 @@
         send("x3", near(3, z, 0), near(3, z, 0), xpart)
 
     def send_ffn():
-        send("x4", up.at[rows_of(512, z, 0), :], far(4, z, 0), xpart)
-        send("x5", down.at[rows_of(128, z, 0), :], far(5, z, 0), xpart)
-
-    def share(k, i, quarter, part):
+        for k, w in ((4, up), (5, down)):
+            size = 256 if k == 4 else 64
+            base = (1 - xl) * 4 * size + z * size
+            send(f"x{k}", w.at[pl.ds(pl.multiple_of(base, size), size), :], far(k, z, 0, 1 - xl), xpart)
+
+    def pass_on(k, i, quarter, part):
         if k >= 4:
-            src = far(k, quarter, part)
-            to = up4 if k == 4 else down4
-            dst = to.at[3, rows_of(512 if k == 4 else 128, quarter, part), :]
-            send(f"s{k}{i}", src, dst, sibling)
+            send(f"n{k}{i}", far(k, quarter, part), far(k, quarter, part), xn)
 
     def pump_x(k):
         await_to(f"x{k}", far(k, z, 0))
         send(f"z{k}+", far(k, z, 0), far(k, z, 0), zp)
         send(f"z{k}-", far(k, z, 0), far(k, z, 0), zm)
-        share(k, 0, z, 0)
+        pass_on(k, 0, z, 0)
 
     def pump_z(k):
         await_to(f"z{k}+", far(k, z + 3, 0))
         send(f"z{k}f+", far(k, z + 3, 1), far(k, z + 3, 1), zp)
-        share(k, 1, z + 3, 0)
+        pass_on(k, 1, z + 3, 0)
         await_to(f"z{k}-", far(k, z + 1, 0))
         send(f"z{k}f-", far(k, z + 1, 2), far(k, z + 1, 2), zm)
-        share(k, 2, z + 1, 0)
+        pass_on(k, 2, z + 1, 0)
 
     def end_z(k):
         await_to(f"z{k}f+", far(k, z + 2, 1))
-        share(k, 3, z + 2, 1)
+        pass_on(k, 3, z + 2, 1)
         await_to(f"z{k}f-", far(k, z + 2, 2))
-        share(k, 4, z + 2, 2)
+        pass_on(k, 4, z + 2, 2)
+
+    def share(k, i):
+        to = up4 if k == 4 else down4
+        rows = half_rows(k, xl if i == 0 else 1 - xl)
+        send(f"s{k}{i}", to.at[2, rows, :], to.at[3, rows, :], sibling)
+
+    def end_n(k):
+        for i, (quarter, part) in enumerate(((z, 0), (z + 3, 0), (z + 1, 0), (z + 2, 1), (z + 2, 2))):
+            await_to(f"n{k}{i}", far(k, quarter, part, 1 - xl))
 
     def pump_r1():
         await_to("yr+1", near(1, z + 1, 0))
@@ -301,6 +330,11 @@
         await_to("yr-2", near(2, z + 2, 0))
         send("yrf2-", near(2, z + 2, 2), near(2, z + 2, 2), ym)
 
+    send("x0", mw.at[rows_of(1024, z, 0), :], near(0, z, 0), xpart)
+    send_own("yq+", z, yp)
+    send_own("yq-", z, ym)
+    send_ffn()
+
     local[0].wait()
 
     def norm_block(i):
@@ -308,6 +342,50 @@
         normed[r, :] = norm_rows(tok[r, :].astype(F32)).astype(BF)
 
     loop(9, norm_block)
+    for n in (6, 3, 4, 5):
+        local[n].start()
+    early.wait()
+
+    def pack(i):
+        packed[:, cols(i, 256)] = jnp.dot(
+            ps[...], normed[:, cols(i, 256)], preferred_element_type=F32
+        ).astype(BF)
+
+    loop(4, pack)
+
+    def hcopy(i, src_at, dst_at, rows, dev):
+        return pltpu.make_async_remote_copy(
+            src_ref=packed.at[pl.ds(src_at, rows), :], dst_ref=halo.at[pl.ds(dst_at, rows), :],
+            send_sem=hs.at[i], recv_sem=hr.at[i], device_id=dev, device_id_type=MESH,
+        )
+
+    middle_sends = [
+        hcopy(0, SEND_W, HALO_E, 112, (lat, west)),
+        hcopy(1, SEND_E, HALO_W, 112, (lat, east)),
+    ]
+    north_sends = [
+        hcopy(2, SEND_N, HALO_S, 80, (lat - 1, lon)),
+        hcopy(3, SEND_N, HALO_SE, 32, (lat - 1, west)),
+        hcopy(4, SEND_N + 48, HALO_SW, 32, (lat - 1, east)),
+    ]
+    south_sends = [
+        hcopy(5, SEND_S, HALO_N, 80, (lat + 1, lon)),
+        hcopy(6, SEND_S, HALO_NE, 32, (lat + 1, west)),
+        hcopy(7, SEND_S + 48, HALO_NW, 32, (lat + 1, east)),
+    ]
+    for cp in middle_sends:
+        cp.start()
+
+    @pl.when(north)
+    def _():
+        for cp in north_sends:
+            cp.start()
+
+    @pl.when(south)
+    def _():
+        for cp in south_sends:
+            cp.start()
+
     local[1].wait()
 
     def permute(i):
@@ -317,55 +395,16 @@
 
     loop(4, permute)
 
-    def hcopy(i, src_at, dst_at, rows, dev):
-        return pltpu.make_async_remote_copy(
-            src_ref=xp.at[pl.ds(src_at, rows), :], dst_ref=halo.at[pl.ds(dst_at, rows), :],
-            send_sem=hs.at[i], recv_sem=hr.at[i], device_id=dev, device_id_type=MESH,
-        )
-
-    at = {k: v[0] for k, v in PIECE.items()}
-    middle_sends = [
-        hcopy(0, 0, HALO_E, 160, (lat, west)),
-        hcopy(1, at[0, 2], HALO_W, 160, (lat, east)),
-    ]
-    north_sends = [
-        hcopy(2, at[0, 0], HALO_S, 32, (lat - 1, lon)),
-        hcopy(3, at[0, 1], HALO_S + 32, 48, (lat - 1, lon)),
-        hcopy(4, at[0, 2], HALO_S + 80, 32, (lat - 1, lon)),
-        hcopy(5, at[0, 0], HALO_SE, 32, (lat - 1, west)),
-        hcopy(6, at[0, 2], HALO_SW, 32, (lat - 1, east)),
-    ]
-    south_sends = [
-        hcopy(7, at[3, 0], HALO_N, 32, (lat + 1, lon)),
-        hcopy(8, at[3, 1], HALO_N + 32, 48, (lat + 1, lon)),
-        hcopy(9, at[3, 2], HALO_N + 80, 32, (lat + 1, lon)),
-        hcopy(10, at[3, 0], HALO_NE, 32, (lat + 1, west)),
-        hcopy(11, at[3, 2], HALO_NW, 32, (lat + 1, east)),
-    ]
-    for cp in middle_sends:
-        cp.start()
-
-    @pl.when(north)
-    def _():
-        for cp in north_sends:
-            cp.start()
-
-    @pl.when(south)
-    def _():
-        for cp in south_sends:
-            cp.start()
-
     @pl.when(jnp.logical_not(north))
     def _():
-        halo[HALO_N : HALO_N + 112, :] = jnp.zeros((112, D), BF)
+        halo[HALO_N : HALO_N + 80, :] = jnp.zeros((80, D), BF)
         halo[HALO_NW : HALO_NW + 64, :] = jnp.zeros((64, D), BF)
 
     @pl.when(jnp.logical_not(south))
     def _():
-        halo[HALO_S : HALO_S + 112, :] = jnp.zeros((112, D), BF)
+        halo[HALO_S : HALO_S + 80, :] = jnp.zeros((80, D), BF)
         halo[HALO_SW : HALO_SW + 64, :] = jnp.zeros((64, D), BF)
 
-    pump_y()
     local[2].wait()
 
     def project(i):
@@ -373,53 +412,33 @@
             xp[...], qkvv[:, cols(i, 256)], preferred_element_type=F32
         ).astype(BF)
 
-    loop(12, project)
+    def project_late(i):
+        project(i + 6)
+
+    loop(6, project)
+    pump_y()
+    local[7].start()
+    local[8].start()
+    loop(6, project_late)
     pump_x(0)
-    pump_y2()
     send("up", up, up4.at[1], sibling)
     send("down", down, down4.at[1], sibling)
 
-    for cp in middle_sends:
-        cp.wait()
-
-    @pl.when(north)
-    def _():
-        for cp in south_sends:
-            cp.wait_recv()
-        for cp in north_sends:
-            cp.wait_send()
-
-    @pl.when(south)
-    def _():
-        for cp in north_sends:
-            cp.wait_recv()
-        for cp in south_sends:
-            cp.wait_send()
-
-    def project_halo(i):
-        kvh[:, cols(i, 256)] = jnp.dot(
-            halo[...], qkvv[:, cols(i, 256, D)], preferred_element_type=F32
-        ).astype(BF)
-
-    loop(8, project_halo)
-    pump_x(1)
-    pump_x(2)
-    pump_z(0)
-
     edge = jnp.where(north, jnp.where(south, 0, 2), 1)
     low = lax.broadcasted_iota(jnp.int32, (1, 128), 1) < 64
-    att = xp
-
-    def pair(i):
+
+    def attend(i, inner):
         head = cols(i, 128)
         head_k, head_v = cols(i, 128, D), cols(i, 128, 2 * D)
         for w, ((start, rows, _), parts) in enumerate(WINDOWS):
+            if inner == bool(parts):
+                continue
             r = slice(start, start + rows)
             q = qkv[r, head] * jnp.asarray(0.125, BF)
             zero = jnp.zeros_like(q)
             q = jnp.concatenate([jnp.where(low, q, zero), jnp.where(low, zero, q)], axis=0)
             ks, vs = [qkv[r, head_k]], [qkv[r, head_v]]
-            for off, prows, _, _ in parts:
+            for off, prows, _, _, _ in parts:
                 ks.append(kvh[off : off + prows, head])
                 vs.append(kvh[off : off + prows, head_k])
             k = jnp.concatenate(ks, axis=0) if parts else ks[0]
@@ -434,17 +453,61 @@
             den = jnp.where(low, o[:rows, 128:], o[rows:, 128:])
             att[r, head] = (num / den).astype(BF)
 
-    def pair_late(i):
-        pair(i + 4)
-
-    loop(4, pair)
+    att = xp
+
+    def pair_inner(i):
+        attend(i, True)
+
+    loop(8, pair_inner)
+    pump_y2()
+
+    for cp in middle_sends:
+        cp.wait()
+
+    @pl.when(north)
+    def _():
+        for cp in south_sends:
+            cp.wait_recv()
+        for cp in north_sends:
+            cp.wait_send()
+
+    @pl.when(south)
+    def _():
+        for cp in north_sends:
+            cp.wait_recv()
+        for cp in south_sends:
+            cp.wait_send()
+
+    def project_halo(i):
+        kvh[:, cols(i, 256)] = jnp.dot(
+            halo[...], qkvv[:, cols(i, 256, D)], preferred_element_type=F32
+        ).astype(BF)
+
+    loop(8, project_halo)
+    pump_x(1)
+    pump_x(2)
+    pump_x(4)
+    pump_x(5)
+    pump_z(0)
+
+    def quarter_of(n):
+        def pair(i):
+            attend(i + 2 * n, False)
+
+        return pair
+
+    loop(2, quarter_of(0))
     pump_x(3)
     pump_r1()
+    loop(2, quarter_of(1))
     pump_z(1)
-    send_ffn()
-    loop(4, pair_late)
+    pump_z(4)
+    loop(2, quarter_of(2))
     pump_z(2)
+    pump_z(5)
     pump_r2()
+    loop(2, quarter_of(3))
+    pump_z(3)
 
     local[3].wait()
     attr = normed
@@ -464,7 +527,10 @@
     loop(4, out_project)
     store_mid = pltpu.make_async_copy(mid, mid_out, lsem.at[9])
     store_mid.start()
-    pump_z(3)
+    end_z(4)
+    share(4, 0)
+    end_z(5)
+    share(5, 0)
     local[5].wait()
 
     def patch(i):
@@ -493,31 +559,42 @@
     await_to("yrf3", near(3, z + 3, 0))
     await_to("yrf2+", near(3, z + 2, 1))
     await_to("yrf2-", near(3, z + 2, 2))
-    for k in range(4):
-        end_z(k)
-    pump_x(4)
-    pump_x(5)
     keep_mgd.wait()
     theirs_rows = pl.ds(pl.multiple_of((1 - c) * GROUP, 16), GROUP)
     await_to("merged", xs.at[theirs_rows, :])
 
-    def merge(i):
-        v = jnp.zeros((2 * GROUP, 256), F32)
-        for g in range(4):
-            r = slice(g * D, (g + 1) * D)
-            w = jnp.concatenate([wv[2 * i, r, :], wv[2 * i + 1, r, :]], axis=1)
-            v += jnp.dot(xs[:, r], w, preferred_element_type=F32)
-        v = v.astype(BF)
-        cc[0, :, cols(i, 256)] = v[:GROUP]
-        cc[1, :, cols(i, 256)] = v[GROUP:]
-
-    loop(4, merge)
-    send("swap", cc.at[1 - c], theirs, sibling)
-    for j in range(8):
-        coarse[:, pl.ds(pl.multiple_of((2 * j + c) * 128, 128), 128)] = cc[c, :, j * 128 : (j + 1) * 128]
-    await_to("swap", theirs)
-    for j in range(8):
-        coarse[:, pl.ds(pl.multiple_of((2 * j + 1 - c) * 128, 128), 128)] = theirs[:, j * 128 : (j + 1) * 128]
+    def merge_of(n):
+        h = xh if n == 0 else 1 - xh
+
+        def merge(i):
+            v = jnp.zeros((2 * GROUP, 256), F32)
+            for g in range(4):
+                r = slice(g * D, (g + 1) * D)
+                w = jnp.concatenate([wv[4 * i + h, r, :], wv[4 * i + 2 + h, r, :]], axis=1)
+                v += jnp.dot(xs[:, r], w, preferred_element_type=F32)
+            v = v.astype(BF)
+            cc[0, n, :, cols(i, 256)] = v[:GROUP]
+            cc[1, n, :, cols(i, 256)] = v[GROUP:]
+
+        return merge
+
+    def place_columns(n, core, get):
+        h = xh if n == 0 else 1 - xh
+        for j in range(4):
+            at = pl.multiple_of((4 * j + 2 * h + core) * 128, 128)
+            coarse[:, pl.ds(at, 128)] = get(slice(j * 128, (j + 1) * 128))
+
+    loop(2, merge_of(0))
+    send("swap0", cc.at[1 - c, 0], theirs.at[0], sibling)
+    for k in range(4):
+        end_z(k)
+    loop(2, merge_of(1))
+    send("swap1", cc.at[1 - c, 1], theirs.at[1], sibling)
+    for n in (0, 1):
+        place_columns(n, c, lambda t, n=n: cc[c, n, :, t])
+    for n in (0, 1):
+        await_to(f"swap{n}", theirs.at[n])
+        place_columns(n, 1 - c, lambda t, n=n: theirs[n, :, t])
 
     def coarse_norm(i):
         r = pl.ds(pl.multiple_of(i * 16, 16), 16)
@@ -527,8 +604,10 @@
 
     send("ag+", cn.at[0], cn.at[2], yp)
     send("ag-", cn.at[0], cn.at[3], ym)
-    pump_z(4)
-    pump_z(5)
+    end_n(4)
+    share(4, 1)
+    end_n(5)
+    share(5, 1)
     for n in (7, 8):
         local[n].wait()
     await_to("up", up4.at[1])
@@ -563,12 +642,9 @@
     send("ag2+", cn.at[2, A_ROWS, :], cn.at[1, A_ROWS, :], yp)
     await_to("ag-", cn.at[3])
     send("ag2-", cn.at[3, B_ROWS, :], cn.at[1, B_ROWS, :], ym)
-    end_z(4)
-    end_z(5)
-    for k in (4, 5):
-        to, size = (up4, 512) if k == 4 else (down4, 128)
-        for i, (quarter, part) in enumerate(((z, 0), (z + 3, 0), (z + 1, 0), (z + 2, 1), (z + 2, 2))):
-            await_to(f"s{k}{i}", to.at[3, rows_of(size, quarter, part), :])
+    for k, to in ((4, up4), (5, down4)):
+        for i in range(2):
+            await_to(f"s{k}{i}", to.at[3, half_rows(k, xl if i == 0 else 1 - xl), :])
     ffn(2, 2)
     send("rs2", pt.at[2], rb.at[3], ym)
     send("rs3", pt.at[3], rb.at[2], yp)
@@ -604,7 +680,7 @@
 
 
 def per_device(tokens, qkv_weight, out_weight, merge_weight, up_weight, down_weight):
-    order, patch = _tables()
+    order, packed, patch = _tables()
     p1 = jnp.asarray(order, BF)
     p1t = jnp.asarray(order.T, BF)
     pg = jnp.asarray(patch, BF)
@@ -619,10 +695,11 @@
             jax.ShapeDtypeStruct((CELLS, D), BF),
             jax.ShapeDtypeStruct((ROWS // 2, COLS // 2, DC), BF),
         ),
-        in_specs=[HBM, HBM, VM] + [HBM] * 7,
+        in_specs=[HBM, HBM, HBM, VM] + [HBM] * 7,
         out_specs=(HBM, VM),
         scratch_shapes=[
             vmem(CELLS, D),
+            vmem(SENT, CELLS),
             vmem(OWN, CELLS),
             vmem(CELLS, OWN),
             vmem(4 * GROUP, CELLS),
@@ -632,6 +709,7 @@
             vmem(4, DC, 512),
             vmem(4, 512, DC),
             vmem(CELLS, D),
+            vmem(SENT, D),
             vmem(OWN, D),
             vmem(HALO, D),
             vmem(OWN, 3 * D),
@@ -639,15 +717,15 @@
             vmem(CELLS, D),
             vmem(GROUP, 4 * D),
             vmem(2 * GROUP, 4 * D),
-            vmem(2, GROUP, D),
-            vmem(GROUP, D),
+            vmem(2, 2, GROUP, 512),
+            vmem(2, GROUP, 512),
             vmem(GROUP, DC),
             vmem(4, GROUP, DC),
             vmem(2 * GROUP, DC),
             vmem(GROUP, DC, kind=F32),
             vmem(4, GROUP, DC),
             vmem(4, GROUP, DC),
-            DMA((11,)),
+            DMA((12,)),
             DMA((HALO_SENDS,)),
             DMA((HALO_SENDS,)),
             DMA((len(WSEMS),)),
@@ -657,7 +735,7 @@
             collective_id=0, has_side_effects=True, vmem_limit_bytes=62 * 2**20
         ),
     )(
-        tokens.reshape(CELLS, D), p1, jnp.asarray(_bias()), qkv_weight, out_weight, merge_weight, p1t, pg,
+        tokens.reshape(CELLS, D), jnp.asarray(packed, BF), p1, jnp.asarray(_bias()), qkv_weight, out_weight, merge_weight, p1t, pg,
         up_weight, down_weight,
     )
     return mid.reshape(ROWS, COLS, D), coarse_out

time: 140 us -> 143 us (1.021)
  Pallas kernels: 136 us -> 138 us
    pallas_call x1, Pallas kernels: 136 us -> 138 us  [per_device(): pl.pallas_call(kernel, name='whole', out_shape=(jax.ShapeDtypeStruct((CEL...]
where the time goes in v3:
time: 143 us; the launch traced here: 141 us
  Pallas kernels  138 us (97%)
  local copies, waits for them, and re-layouts  3.02 us (2%)
    pallas_call x1, Pallas kernels, per_device(): pl.pallas_call(kernel, name='whole', out_shape=(jax.ShapeDtypeStruct((CEL...  138 us
    unnamed x4, local copies, waits for them, and re-layouts  3.02 us

profile of v3, /device:TPU:1, one launch (start us, length us, event | category | flops | bytes accessed | tf_op | source)
XLA Modules:
  0.0 141.3 jit_solution(14227235614460944313)
XLA Ops:
  0.6 137.6 %whole.1 = (bf16[432,1024]{1,0:T(8,128)(2,1)}, bf16[9,12,2048]{2,1,0:T(8,128)(2,1)}) custom-call(bf16[432,1024]{1,0:T(8,128)(2,1)} %bitcast.3, bf16[384,432]{1,0:T(8,128)(2,1)} %constant.13.clone.ps_in, bf16[576,432]{1,0:T(8,128)(2,1)} %constant.10.clone.p1_in, f32[3,16,128]{2,1,0:T(8,128)} %constant.14.clone.bias, bf16[1024,3072]{1,0:T(8,128)(2,1)} %qkvw.1, ...), custom_call_target="tpu_custom_call" | custom-call | tf_op jit(solution)/shard_map/whole/pallas_call | solution.py:691
  138.3 0.0 copy-start
  138.3 2.2 %copy.15 = bf16[18,24,1024]{2,1,0:T(8,128)(2,1)} copy(bf16[18,24,1024]{2,1,0:T(8,128)(2,1)} %bitcast.2) | data formatting | bytes 1769472
  140.5 0.0 copy-done
  140.5 0.8 copy.16
Async XLA Ops:
  138.3 2.2 %copy-start = (bf16[9,12,2048]{2,1,0:T(8,128)(2,1)S(1)}, bf16[9,12,2048]{2,1,0:T(8,128)(2,1)}, u32[]{:S(2)}) copy-start(bf16[9,12,2048]{2,1,0:T(8,128)(2,1)} %get-tuple-element.9) | copy-start | bytes 1327108

commit v4 on v3

--- a/solution.py
+++ b/solution.py
@@ -136,19 +136,39 @@
 
 
 HALO_SENDS = 8
+ORDER = (
+    ("x00", 3), ("ya+0", 3), ("ya-1", 3), ("ya+1", 7), ("ya-0", 7), ("z00a", 8), ("yb+", 11), ("yb-", 11),
+    ("n00", 11), ("x01", 12), ("yq+", 14), ("yq-", 14), ("x10", 15), ("z00b", 16), ("n01", 17), ("z01a", 17),
+    ("x11", 18), ("ye+", 20), ("ye-", 20), ("n10", 20), ("z10a", 20), ("x20", 21), ("z01b", 22), ("yt+", 23),
+    ("yt-", 23), ("n11", 23), ("x21", 24), ("z10b", 25), ("z11a", 25), ("n20", 26), ("x30", 27), ("z11b", 28),
+    ("z20a", 28), ("yu+", 29), ("yu-", 29), ("n21", 29), ("x31", 30), ("z20b", 31), ("z21a", 31), ("yef+", 32),
+    ("yef-", 32), ("n30", 32), ("x40", 33), ("z21b", 34), ("z30a", 34), ("yqf+", 35), ("yqf-", 35), ("n31", 35),
+    ("x41", 36), ("z30b", 37), ("z31a", 37), ("n40", 38), ("x50", 39), ("z31b", 40), ("z40a", 40), ("n41", 41),
+    ("x51", 42), ("z40b", 43), ("z41a", 43), ("n50", 44), ("x60", 46), ("z41b", 46), ("z50a", 46), ("n51", 48),
+    ("x61", 49), ("z50b", 50), ("z51a", 50), ("n60", 51), ("x70", 52), ("z51b", 53), ("z60a", 53), ("n61", 54),
+    ("x71", 55), ("z60b", 56), ("z61a", 56), ("n70", 57), ("z61b", 59), ("z70a", 59), ("n71", 60), ("z70b", 62),
+    ("z71a", 62), ("z71b", 65),
+)
 WSEMS = {}
 for _n in (
-    ["yq+", "yq-", "yqf+", "yqf-"]
-    + [f"yr{s}{i}" for s in "+-" for i in (1, 2, 3)]
-    + ["yrf1", "yrf3", "yrf2+", "yrf2-"]
-    + [f"x{k}" for k in range(6)]
-    + [f"z{k}{s}" for k in range(6) for s in ("+", "-", "f+", "f-")]
-    + [f"n{k}{i}" for k in (4, 5) for i in range(5)]
-    + [f"s{k}{i}" for k in (4, 5) for i in range(2)]
+    [n for n, _ in ORDER]
+    + [f"s{k}" for k in (4, 5, 6, 7)]
     + ["up", "down", "merged", "swap0", "swap1"]
     + ["ag+", "ag-", "ag2+", "ag2-", "rs1", "rs2", "rs3"]
 ):
     WSEMS[_n] = len(WSEMS)
+
+
+def needs(name):
+    if name[0] in "nz":
+        return [("n" if name[-1] == "b" else "x") + name[1:3]]
+    if name[0] == "x":
+        k, i = int(name[1]), name[2]
+        return {1: [f"ya+{i}"], 2: [f"ya-{i}"], 3: ["yb+" if i == "0" else "yb-"]}.get(k, [])
+    first = {"yb+": "ya+0", "yb-": "ya-1", "yqf+": "yq+", "yqf-": "yq-", "yef+": "ye+", "yef-": "ye-"}
+    return [first[name]] if name in first else []
+
+
 A_ROWS, B_ROWS = pl.ds(0, 64), pl.ds(64, 48)
 
 
@@ -220,11 +240,11 @@
         yy = (y + (0, 3, 1, 2)[k]) % 4
         return 2 * yy + (1 - xh if other else xh)
 
-    def rows_of(size, quarter, part):
-        base = (quarter % 4) * size
-        if part == 0:
-            return pl.ds(pl.multiple_of(base, size), size)
-        return pl.ds(pl.multiple_of(base + (part - 1) * (size // 2), size // 2), size // 2)
+    def rows_of(size, quarter, half, base=0):
+        at = base + (quarter % 4) * 2 * size
+        if half is None:
+            return pl.ds(pl.multiple_of(at, size), 2 * size)
+        return pl.ds(pl.multiple_of(at + half * size, size), size)
 
     sends = {}
 
@@ -242,98 +262,100 @@
     def await_to(name, dst):
         remote(name, dst, dst, yp).wait_recv()
 
-    def near(k, quarter, part):
-        return wv.at[block(k, False), rows_of(1024, quarter, part), :]
-
-    def send_own(name, quarter, dev):
-        send(name, mw.at[rows_of(1024, quarter, 0), :], near(0, quarter, 0), dev)
-
-    def far(k, quarter, part, half=xl):
+    def near(k, quarter, half):
+        return wv.at[block(k, False), rows_of(512, quarter, half), :]
+
+    def far_rows(k, quarter, half):
+        if k < 6:
+            return rows_of(128, quarter, half, (k - 4) * 1024)
+        return rows_of(32, quarter, half, (k - 6) * 256)
+
+    def far(k, quarter, half):
         if k < 4:
-            return wv.at[block(k, True), rows_of(1024, quarter, part), :]
-        size = 256 if k == 4 else 64
-        base = (quarter % 4) * size + half * 4 * size
-        if part == 0:
-            rows = pl.ds(pl.multiple_of(base, size), size)
+            return wv.at[block(k, True), rows_of(512, quarter, half), :]
+        return (up4 if k < 6 else down4).at[2, far_rows(k, quarter, half), :]
+
+    ox = 1 - xl
+
+    def region(name):
+        kind, sign = name[:-2] if name[1] == "a" else name[:-1], name[2] if name[1] == "a" else name[-1]
+        plus = sign == "+"
+        if kind == "ya":
+            return z + int(name[3]), ox
+        if kind == "yb":
+            return (z, ox) if plus else (z + 1, ox)
+        if kind in ("yq", "yqf"):
+            return (z + 2, None) if plus else (z + 3, None)
+        if kind == "yt":
+            return (z + 3, None) if plus else (z + 2, None)
+        if kind in ("ye", "yef"):
+            return (z, xl) if plus else (z + 1, xl)
+        return (z + 1, xl) if plus else (z, xl)
+
+    def landing(name):
+        if name[0] == "y":
+            second = name[:2] == "yb" or name[:3] in ("yqf", "yef")
+            k = 3 if second else 1 if "+" in name else 2
+            return near(k, *region(name))
+        k, i = int(name[1]), int(name[2])
+        if name[0] == "x":
+            return far(k, z + i, xl)
+        if name[0] == "n":
+            return far(k, z + i, ox)
+        return far(k, z + 3 if i == 0 else z + 2, xl if name[3] == "a" else ox)
+
+    def start(name):
+        if name[0] == "y":
+            plus = "+" in name
+            dev = yp if plus else ym
+            if name[:2] == "yb" or name[:3] in ("yqf", "yef"):
+                ref = near(1 if plus else 2, *region(name))
+                send(name, ref, ref, dev)
+            else:
+                quarter, half = region(name)
+                send(name, mw.at[rows_of(512, quarter, half), :], near(0, quarter, half), dev)
+            return
+        k, i = int(name[1]), int(name[2])
+        if name[0] == "x":
+            if k == 0:
+                send(name, mw.at[rows_of(512, z + i, ox), :], near(0, z + i, ox), xpart)
+            elif k < 4:
+                send(name, near(k, z + i, ox), near(k, z + i, ox), xpart)
+            else:
+                send(name, (up if k < 6 else down).at[far_rows(k, z + i, ox), :], far(k, z + i, ox), xpart)
+        elif name[0] == "n":
+            send(name, far(k, z + i, xl), far(k, z + i, xl), xn)
         else:
-            rows = pl.ds(pl.multiple_of(base + (part - 1) * (size // 2), size // 2), size // 2)
-        return (up4 if k == 4 else down4).at[2, rows, :]
-
-    def half_rows(k, half):
-        size = 1024 if k == 4 else 256
-        return pl.ds(pl.multiple_of(half * size, size), size)
-
-    def pump_y():
-        await_to("yq+", near(1, z, 0))
-        send("yqf+", near(1, z, 1), near(1, z, 1), yp)
-        send("x1", near(1, z, 0), near(1, z, 0), xpart)
-        await_to("yq-", near(2, z, 0))
-        send("yqf-", near(2, z, 2), near(2, z, 2), ym)
-        send("x2", near(2, z, 0), near(2, z, 0), xpart)
-        for i in (1, 3, 2):
-            send_own(f"yr+{i}", z + i, yp)
-            send_own(f"yr-{i}", z + i, ym)
-
-    def pump_y2():
-        await_to("yqf+", near(3, z, 1))
-        await_to("yqf-", near(3, z, 2))
-        send("x3", near(3, z, 0), near(3, z, 0), xpart)
-
-    def send_ffn():
-        for k, w in ((4, up), (5, down)):
-            size = 256 if k == 4 else 64
-            base = (1 - xl) * 4 * size + z * size
-            send(f"x{k}", w.at[pl.ds(pl.multiple_of(base, size), size), :], far(k, z, 0, 1 - xl), xpart)
-
-    def pass_on(k, i, quarter, part):
-        if k >= 4:
-            send(f"n{k}{i}", far(k, quarter, part), far(k, quarter, part), xn)
-
-    def pump_x(k):
-        await_to(f"x{k}", far(k, z, 0))
-        send(f"z{k}+", far(k, z, 0), far(k, z, 0), zp)
-        send(f"z{k}-", far(k, z, 0), far(k, z, 0), zm)
-        pass_on(k, 0, z, 0)
-
-    def pump_z(k):
-        await_to(f"z{k}+", far(k, z + 3, 0))
-        send(f"z{k}f+", far(k, z + 3, 1), far(k, z + 3, 1), zp)
-        pass_on(k, 1, z + 3, 0)
-        await_to(f"z{k}-", far(k, z + 1, 0))
-        send(f"z{k}f-", far(k, z + 1, 2), far(k, z + 1, 2), zm)
-        pass_on(k, 2, z + 1, 0)
-
-    def end_z(k):
-        await_to(f"z{k}f+", far(k, z + 2, 1))
-        pass_on(k, 3, z + 2, 1)
-        await_to(f"z{k}f-", far(k, z + 2, 2))
-        pass_on(k, 4, z + 2, 2)
-
-    def share(k, i):
-        to = up4 if k == 4 else down4
-        rows = half_rows(k, xl if i == 0 else 1 - xl)
-        send(f"s{k}{i}", to.at[2, rows, :], to.at[3, rows, :], sibling)
-
-    def end_n(k):
-        for i, (quarter, part) in enumerate(((z, 0), (z + 3, 0), (z + 1, 0), (z + 2, 1), (z + 2, 2))):
-            await_to(f"n{k}{i}", far(k, quarter, part, 1 - xl))
-
-    def pump_r1():
-        await_to("yr+1", near(1, z + 1, 0))
-        send("yrf1", near(1, z + 1, 0), near(1, z + 1, 0), yp)
-        await_to("yr-3", near(2, z + 3, 0))
-        send("yrf3", near(2, z + 3, 0), near(2, z + 3, 0), ym)
-
-    def pump_r2():
-        await_to("yr+2", near(1, z + 2, 0))
-        send("yrf2+", near(1, z + 2, 1), near(1, z + 2, 1), yp)
-        await_to("yr-2", near(2, z + 2, 0))
-        send("yrf2-", near(2, z + 2, 2), near(2, z + 2, 2), ym)
-
-    send("x0", mw.at[rows_of(1024, z, 0), :], near(0, z, 0), xpart)
-    send_own("yq+", z, yp)
-    send_own("yq-", z, ym)
-    send_ffn()
+            ref = far(k, z + i, xl if name[3] == "a" else ox)
+            send(name, ref, ref, zp if i == 0 else zm)
+
+    landed = set()
+    queue = list(ORDER)
+
+    def need(name):
+        if name not in landed:
+            landed.add(name)
+            await_to(name, landing(name))
+
+    def pump(time):
+        while queue and queue[0][1] <= time:
+            name = queue.pop(0)[0]
+            for other in needs(name):
+                need(other)
+            start(name)
+
+    def need_far(k):
+        for n, _ in ORDER:
+            if n[0] in "xnz" and n[1] == str(k):
+                need(n)
+
+    def share(k):
+        size = 1024 if k < 6 else 256
+        rows = pl.ds((k % 2) * size, size)
+        to = up4 if k < 6 else down4
+        send(f"s{k}", to.at[2, rows, :], to.at[3, rows, :], sibling)
+
+    pump(3)
 
     local[0].wait()
 
@@ -412,15 +434,21 @@
             xp[...], qkvv[:, cols(i, 256)], preferred_element_type=F32
         ).astype(BF)
 
+    def project_mid(i):
+        project(i + 4)
+
     def project_late(i):
-        project(i + 6)
-
-    loop(6, project)
-    pump_y()
+        project(i + 8)
+
+    pump(8)
+    loop(4, project)
+    pump(11)
     local[7].start()
     local[8].start()
-    loop(6, project_late)
-    pump_x(0)
+    loop(4, project_mid)
+    pump(13)
+    loop(4, project_late)
+    pump(14)
     send("up", up, up4.at[1], sibling)
     send("down", down, down4.at[1], sibling)
 
@@ -459,7 +487,7 @@
         attend(i, True)
 
     loop(8, pair_inner)
-    pump_y2()
+    pump(16)
 
     for cp in middle_sends:
         cp.wait()
@@ -484,11 +512,7 @@
         ).astype(BF)
 
     loop(8, project_halo)
-    pump_x(1)
-    pump_x(2)
-    pump_x(4)
-    pump_x(5)
-    pump_z(0)
+    pump(20)
 
     def quarter_of(n):
         def pair(i):
@@ -497,17 +521,13 @@
         return pair
 
     loop(2, quarter_of(0))
-    pump_x(3)
-    pump_r1()
+    pump(23)
     loop(2, quarter_of(1))
-    pump_z(1)
-    pump_z(4)
+    pump(25)
     loop(2, quarter_of(2))
-    pump_z(2)
-    pump_z(5)
-    pump_r2()
+    pump(28)
     loop(2, quarter_of(3))
-    pump_z(3)
+    pump(30)
 
     local[3].wait()
     attr = normed
@@ -527,10 +547,7 @@
     loop(4, out_project)
     store_mid = pltpu.make_async_copy(mid, mid_out, lsem.at[9])
     store_mid.start()
-    end_z(4)
-    share(4, 0)
-    end_z(5)
-    share(5, 0)
+    pump(33)
     local[5].wait()
 
     def patch(i):
@@ -552,13 +569,13 @@
     keep_mgd = pltpu.make_async_copy(mgd, xs.at[mine, :], lsem.at[10])
     keep_mgd.start()
 
+    pump(38)
     local[6].wait()
-    await_to("yr+3", near(1, z + 3, 0))
-    await_to("yr-1", near(2, z + 1, 0))
-    await_to("yrf1", near(3, z + 1, 0))
-    await_to("yrf3", near(3, z + 3, 0))
-    await_to("yrf2+", near(3, z + 2, 1))
-    await_to("yrf2-", near(3, z + 2, 2))
+    pump(40)
+    for n, _ in ORDER:
+        if n[0] == "y":
+            need(n)
+    pump(42)
     keep_mgd.wait()
     theirs_rows = pl.ds(pl.multiple_of((1 - c) * GROUP, 16), GROUP)
     await_to("merged", xs.at[theirs_rows, :])
@@ -586,10 +603,12 @@
 
     loop(2, merge_of(0))
     send("swap0", cc.at[1 - c, 0], theirs.at[0], sibling)
+    pump(45)
     for k in range(4):
-        end_z(k)
+        need_far(k)
     loop(2, merge_of(1))
     send("swap1", cc.at[1 - c, 1], theirs.at[1], sibling)
+    pump(48)
     for n in (0, 1):
         place_columns(n, c, lambda t, n=n: cc[c, n, :, t])
     for n in (0, 1):
@@ -604,10 +623,9 @@
 
     send("ag+", cn.at[0], cn.at[2], yp)
     send("ag-", cn.at[0], cn.at[3], ym)
-    end_n(4)
-    share(4, 1)
-    end_n(5)
-    share(5, 1)
+    pump(57)
+    need_far(4)
+    share(4)
     for n in (7, 8):
         local[n].wait()
     await_to("up", up4.at[1])
@@ -642,9 +660,13 @@
     send("ag2+", cn.at[2, A_ROWS, :], cn.at[1, A_ROWS, :], yp)
     await_to("ag-", cn.at[3])
     send("ag2-", cn.at[3, B_ROWS, :], cn.at[1, B_ROWS, :], ym)
-    for k, to in ((4, up4), (5, down4)):
-        for i in range(2):
-            await_to(f"s{k}{i}", to.at[3, half_rows(k, xl if i == 0 else 1 - xl), :])
+    pump(99)
+    for k in (5, 6, 7):
+        need_far(k)
+        share(k)
+    for k in (4, 5, 6, 7):
+        size = 1024 if k < 6 else 256
+        await_to(f"s{k}", (up4 if k < 6 else down4).at[3, pl.ds((k % 2) * size, size), :])
     ffn(2, 2)
     send("rs2", pt.at[2], rb.at[3], ym)
     send("rs3", pt.at[3], rb.at[2], yp)

time: 143 us -> 135 us (0.944); the launches traced: 141 us -> 135 us
  Pallas kernels: 138 us -> 131 us
    pallas_call x1, Pallas kernels: 138 us -> 131 us  [per_device(): pl.pallas_call(kernel, name='whole', out_shape=(jax.ShapeDtypeStruct((CEL...]
where the time goes in v4:
time: 135 us
  Pallas kernels  131 us (97%)
  local copies, waits for them, and re-layouts  3.02 us (2%)
    pallas_call x1, Pallas kernels, per_device(): pl.pallas_call(kernel, name='whole', out_shape=(jax.ShapeDtypeStruct((CEL...  131 us
    unnamed x4, local copies, waits for them, and re-layouts  3.02 us

profile of v4, /device:TPU:1, one launch (start us, length us, event | category | flops | bytes accessed | tf_op | source)
XLA Modules:
  0.0 135.1 jit_solution(2735215557710625516)
XLA Ops:
  0.6 131.4 %whole.1 = (bf16[432,1024]{1,0:T(8,128)(2,1)}, bf16[9,12,2048]{2,1,0:T(8,128)(2,1)}) custom-call(bf16[432,1024]{1,0:T(8,128)(2,1)} %bitcast.3, bf16[384,432]{1,0:T(8,128)(2,1)} %constant.13.clone.ps_in, bf16[576,432]{1,0:T(8,128)(2,1)} %constant.10.clone.p1_in, f32[3,16,128]{2,1,0:T(8,128)} %constant.14.clone.bias, bf16[1024,3072]{1,0:T(8,128)(2,1)} %qkvw.1, ...), custom_call_target="tpu_custom_call" | custom-call | tf_op jit(solution)/shard_map/whole/pallas_call | solution.py:713
  132.1 0.0 copy-start
  132.1 2.2 %copy.15 = bf16[18,24,1024]{2,1,0:T(8,128)(2,1)} copy(bf16[18,24,1024]{2,1,0:T(8,128)(2,1)} %bitcast.2) | data formatting | bytes 1769472
  134.3 0.0 copy-done
  134.3 0.8 copy.16
Async XLA Ops:
  132.1 2.2 %copy-start = (bf16[9,12,2048]{2,1,0:T(8,128)(2,1)S(1)}, bf16[9,12,2048]{2,1,0:T(8,128)(2,1)}, u32[]{:S(2)}) copy-start(bf16[9,12,2048]{2,1,0:T(8,128)(2,1)} %get-tuple-element.9) | copy-start | bytes 1327108

commit v5 on v4

--- a/solution.py
+++ b/solution.py
@@ -236,12 +236,15 @@
     count = len(partners) + jnp.where(north, 3, 0) + jnp.where(south, 3, 0)
     pl.semaphore_wait(barrier, count)
 
+    shift = [2 * ((y + d) % 4) for d in (0, 3, 1, 2)]
+    slots = {False: [v + xh for v in shift], True: [v + 1 - xh for v in shift]}
+    zq = [(z + d) % 4 for d in range(4)]
+
     def block(k, other):
-        yy = (y + (0, 3, 1, 2)[k]) % 4
-        return 2 * yy + (1 - xh if other else xh)
+        return slots[other][k]
 
     def rows_of(size, quarter, half, base=0):
-        at = base + (quarter % 4) * 2 * size
+        at = base + quarter * 2 * size
         if half is None:
             return pl.ds(pl.multiple_of(at, size), 2 * size)
         return pl.ds(pl.multiple_of(at + half * size, size), size)
@@ -255,9 +258,16 @@
             device_id=dev, device_id_type=MESH,
         )
 
-    def send(name, src, dst, dev):
-        sends[name] = remote(name, src, dst, dev)
-        sends[name].start()
+    def send(name, src, dst, dev, like=None):
+        remote(name, src, dst, dev).start()
+        if like is None:
+            rows, width = dst.shape
+            buffer = {128: wv, 512: up4, DC: down4}[width]
+
+            def like():
+                return buffer.at[0, pl.ds(0, rows), :]
+
+        sends[name] = like
 
     def await_to(name, dst):
         remote(name, dst, dst, yp).wait_recv()
@@ -281,16 +291,16 @@
         kind, sign = name[:-2] if name[1] == "a" else name[:-1], name[2] if name[1] == "a" else name[-1]
         plus = sign == "+"
         if kind == "ya":
-            return z + int(name[3]), ox
+            return zq[int(name[3])], ox
         if kind == "yb":
-            return (z, ox) if plus else (z + 1, ox)
+            return (zq[0], ox) if plus else (zq[1], ox)
         if kind in ("yq", "yqf"):
-            return (z + 2, None) if plus else (z + 3, None)
+            return (zq[2], None) if plus else (zq[3], None)
         if kind == "yt":
-            return (z + 3, None) if plus else (z + 2, None)
+            return (zq[3], None) if plus else (zq[2], None)
         if kind in ("ye", "yef"):
-            return (z, xl) if plus else (z + 1, xl)
-        return (z + 1, xl) if plus else (z, xl)
+            return (zq[0], xl) if plus else (zq[1], xl)
+        return (zq[1], xl) if plus else (zq[0], xl)
 
     def landing(name):
         if name[0] == "y":
@@ -299,10 +309,10 @@
             return near(k, *region(name))
         k, i = int(name[1]), int(name[2])
         if name[0] == "x":
-            return far(k, z + i, xl)
+            return far(k, zq[i], xl)
         if name[0] == "n":
-            return far(k, z + i, ox)
-        return far(k, z + 3 if i == 0 else z + 2, xl if name[3] == "a" else ox)
+            return far(k, zq[i], ox)
+        return far(k, zq[3 if i == 0 else 2], xl if name[3] == "a" else ox)
 
     def start(name):
         if name[0] == "y":
@@ -318,15 +328,15 @@
         k, i = int(name[1]), int(name[2])
         if name[0] == "x":
             if k == 0:
-                send(name, mw.at[rows_of(512, z + i, ox), :], near(0, z + i, ox), xpart)
+                send(name, mw.at[rows_of(512, zq[i], ox), :], near(0, zq[i], ox), xpart)
             elif k < 4:
-                send(name, near(k, z + i, ox), near(k, z + i, ox), xpart)
+                send(name, near(k, zq[i], ox), near(k, zq[i], ox), xpart)
             else:
-                send(name, (up if k < 6 else down).at[far_rows(k, z + i, ox), :], far(k, z + i, ox), xpart)
+                send(name, (up if k < 6 else down).at[far_rows(k, zq[i], ox), :], far(k, zq[i], ox), xpart)
         elif name[0] == "n":
-            send(name, far(k, z + i, xl), far(k, z + i, xl), xn)
+            send(name, far(k, zq[i], xl), far(k, zq[i], xl), xn)
         else:
-            ref = far(k, z + i, xl if name[3] == "a" else ox)
+            ref = far(k, zq[i], xl if name[3] == "a" else ox)
             send(name, ref, ref, zp if i == 0 else zm)
 
     landed = set()
@@ -336,6 +346,13 @@
         if name not in landed:
             landed.add(name)
             await_to(name, landing(name))
+
+    def pump_at(i, steps):
+        for n, time in steps.items():
+
+            @pl.when(i == n)
+            def _(time=time):
+                pump(time)
 
     def pump(time):
         while queue and queue[0][1] <= time:
@@ -353,7 +370,7 @@
         size = 1024 if k < 6 else 256
         rows = pl.ds((k % 2) * size, size)
         to = up4 if k < 6 else down4
-        send(f"s{k}", to.at[2, rows, :], to.at[3, rows, :], sibling)
+        send(f"s{k}", to.at[2, rows, :], to.at[3, rows, :], sibling, lambda: to.at[3, rows, :])
 
     pump(3)
 
@@ -433,24 +450,15 @@
         qkv[:, cols(i, 256)] = jnp.dot(
             xp[...], qkvv[:, cols(i, 256)], preferred_element_type=F32
         ).astype(BF)
-
-    def project_mid(i):
-        project(i + 4)
-
-    def project_late(i):
-        project(i + 8)
-
-    pump(8)
-    loop(4, project)
-    pump(11)
+        pump_at(i, {3: 10, 7: 12})
+
     local[7].start()
     local[8].start()
-    loop(4, project_mid)
-    pump(13)
-    loop(4, project_late)
+    pump(8)
+    loop(12, project)
     pump(14)
-    send("up", up, up4.at[1], sibling)
-    send("down", down, down4.at[1], sibling)
+    send("up", up, up4.at[1], sibling, lambda: up4.at[1])
+    send("down", down, down4.at[1], sibling, lambda: down4.at[1])
 
     edge = jnp.where(north, jnp.where(south, 0, 2), 1)
     low = lax.broadcasted_iota(jnp.int32, (1, 128), 1) < 64
@@ -459,8 +467,7 @@
         head = cols(i, 128)
         head_k, head_v = cols(i, 128, D), cols(i, 128, 2 * D)
         for w, ((start, rows, _), parts) in enumerate(WINDOWS):
-            if inner == bool(parts):
-                continue
+            if inner: continue
             r = slice(start, start + rows)
             q = qkv[r, head] * jnp.asarray(0.125, BF)
             zero = jnp.zeros_like(q)
@@ -486,7 +493,6 @@
     def pair_inner(i):
         attend(i, True)
 
-    loop(8, pair_inner)
     pump(16)
 
     for cp in middle_sends:
@@ -511,23 +517,15 @@
             halo[...], qkvv[:, cols(i, 256, D)], preferred_element_type=F32
         ).astype(BF)
 
+    pump(20)
     loop(8, project_halo)
-    pump(20)
-
-    def quarter_of(n):
-        def pair(i):
-            attend(i + 2 * n, False)
-
-        return pair
-
-    loop(2, quarter_of(0))
-    pump(23)
-    loop(2, quarter_of(1))
-    pump(25)
-    loop(2, quarter_of(2))
-    pump(28)
-    loop(2, quarter_of(3))
-    pump(30)
+    pump(22)
+
+    def pair_outer(i):
+        attend(i, False)
+        pump_at(i, {0: 24, 1: 26, 2: 27, 3: 29, 4: 31, 5: 33, 6: 34, 7: 36})
+
+    loop(8, pair_outer)
 
     local[3].wait()
     attr = normed
@@ -547,7 +545,7 @@
     loop(4, out_project)
     store_mid = pltpu.make_async_copy(mid, mid_out, lsem.at[9])
     store_mid.start()
-    pump(33)
+    pump(38)
     local[5].wait()
 
     def patch(i):
@@ -565,13 +563,12 @@
 
     loop(GROUP // 16, merge_norm)
     mine = pl.ds(pl.multiple_of(c * GROUP, 16), GROUP)
-    send("merged", mgd, xs.at[mine, :], sibling)
+    send("merged", mgd, xs.at[mine, :], sibling, lambda: mgd)
     keep_mgd = pltpu.make_async_copy(mgd, xs.at[mine, :], lsem.at[10])
     keep_mgd.start()
 
-    pump(38)
+    pump(40)
     local[6].wait()
-    pump(40)
     for n, _ in ORDER:
         if n[0] == "y":
             need(n)
@@ -580,20 +577,26 @@
     theirs_rows = pl.ds(pl.multiple_of((1 - c) * GROUP, 16), GROUP)
     await_to("merged", xs.at[theirs_rows, :])
 
-    def merge_of(n):
-        h = xh if n == 0 else 1 - xh
-
-        def merge(i):
-            v = jnp.zeros((2 * GROUP, 256), F32)
-            for g in range(4):
-                r = slice(g * D, (g + 1) * D)
-                w = jnp.concatenate([wv[4 * i + h, r, :], wv[4 * i + 2 + h, r, :]], axis=1)
-                v += jnp.dot(xs[:, r], w, preferred_element_type=F32)
-            v = v.astype(BF)
-            cc[0, n, :, cols(i, 256)] = v[:GROUP]
-            cc[1, n, :, cols(i, 256)] = v[GROUP:]
-
-        return merge
+    def merge(i):
+        n = i // 2
+
+        @pl.when(i == 2)
+        def _():
+            send("swap0", cc.at[1 - c, 0], theirs.at[0], sibling, lambda: theirs.at[0])
+            pump(45)
+            for k in range(4):
+                need_far(k)
+
+        h = jnp.where(n == 0, xh, 1 - xh)
+        first = 4 * (i % 2) + h
+        v = jnp.zeros((2 * GROUP, 256), F32)
+        for g in range(4):
+            r = slice(g * D, (g + 1) * D)
+            w = jnp.concatenate([wv[first, r, :], wv[first + 2, r, :]], axis=1)
+            v += jnp.dot(xs[:, r], w, preferred_element_type=F32)
+        v = v.astype(BF)
+        cc[0, n, :, cols(i % 2, 256)] = v[:GROUP]
+        cc[1, n, :, cols(i % 2, 256)] = v[GROUP:]
 
     def place_columns(n, core, get):
         h = xh if n == 0 else 1 - xh
@@ -601,13 +604,8 @@
             at = pl.multiple_of((4 * j + 2 * h + core) * 128, 128)
             coarse[:, pl.ds(at, 128)] = get(slice(j * 128, (j + 1) * 128))
 
-    loop(2, merge_of(0))
-    send("swap0", cc.at[1 - c, 0], theirs.at[0], sibling)
-    pump(45)
-    for k in range(4):
-        need_far(k)
-    loop(2, merge_of(1))
-    send("swap1", cc.at[1 - c, 1], theirs.at[1], sibling)
+    loop(4, merge)
+    send("swap1", cc.at[1 - c, 1], theirs.at[1], sibling, lambda: theirs.at[1])
     pump(48)
     for n in (0, 1):
         place_columns(n, c, lambda t, n=n: cc[c, n, :, t])
@@ -621,8 +619,8 @@
 
     loop(GROUP // 16, coarse_norm)
 
-    send("ag+", cn.at[0], cn.at[2], yp)
-    send("ag-", cn.at[0], cn.at[3], ym)
+    send("ag+", cn.at[0], cn.at[2], yp, lambda: cn.at[2])
+    send("ag-", cn.at[0], cn.at[3], ym, lambda: cn.at[3])
     pump(57)
     need_far(4)
     share(4)
@@ -631,14 +629,15 @@
     await_to("up", up4.at[1])
     await_to("down", down4.at[1])
 
-    def ffn(first, count):
-        rows = count * GROUP
+    def ffn(n):
+        first = 2 - 2 * n
+        rows = 2 * GROUP
 
         def up_step(i):
             q, t = i // 2, i % 2
-            x = cn[first : first + count].reshape(rows, DC)
+            x = cn[pl.ds(first, 2)].reshape(rows, DC)
             h = jnp.dot(x, up4[q, :, cols(t, 256)], preferred_element_type=F32)
-            hid[:rows, cols(i, 256)] = gelu(h).astype(BF)
+            hid[:, cols(i, 256)] = gelu(h).astype(BF)
 
         loop(8, up_step)
 
@@ -646,20 +645,24 @@
             t = cols(i, 256)
             v = jnp.zeros((rows, 256), F32)
             for q in range(4):
-                v += jnp.dot(hid[:rows, q * 512 : (q + 1) * 512], down4[q, :, t], preferred_element_type=F32)
-            for n in range(count):
-                part = v[n * GROUP : (n + 1) * GROUP]
-                if first + n == 0:
-                    acc[:, t] = part + coarse[:, t].astype(F32)
-                else:
-                    pt[first + n, :, t] = part.astype(BF)
+                v += jnp.dot(hid[:, q * 512 : (q + 1) * 512], down4[q, :, t], preferred_element_type=F32)
+            acc[:, t] = v[:GROUP] + coarse[:, t].astype(F32)
+            pt[first, :, t] = v[:GROUP].astype(BF)
+            pt[first + 1, :, t] = v[GROUP:].astype(BF)
 
         loop(8, down_step)
 
+        @pl.when(n == 0)
+        def _():
+            send("rs2", pt.at[2], rb.at[3], ym, lambda: rb.at[3])
+            send("rs3", pt.at[3], rb.at[2], yp, lambda: rb.at[2])
+            await_to("ag2+", cn.at[1, A_ROWS, :])
+            await_to("ag2-", cn.at[1, B_ROWS, :])
+
     await_to("ag+", cn.at[2])
-    send("ag2+", cn.at[2, A_ROWS, :], cn.at[1, A_ROWS, :], yp)
+    send("ag2+", cn.at[2, A_ROWS, :], cn.at[1, A_ROWS, :], yp, lambda: cn.at[1, A_ROWS, :])
     await_to("ag-", cn.at[3])
-    send("ag2-", cn.at[3, B_ROWS, :], cn.at[1, B_ROWS, :], ym)
+    send("ag2-", cn.at[3, B_ROWS, :], cn.at[1, B_ROWS, :], ym, lambda: cn.at[1, B_ROWS, :])
     pump(99)
     for k in (5, 6, 7):
         need_far(k)
@@ -667,13 +670,8 @@
     for k in (4, 5, 6, 7):
         size = 1024 if k < 6 else 256
         await_to(f"s{k}", (up4 if k < 6 else down4).at[3, pl.ds((k % 2) * size, size), :])
-    ffn(2, 2)
-    send("rs2", pt.at[2], rb.at[3], ym)
-    send("rs3", pt.at[3], rb.at[2], yp)
-    await_to("ag2+", cn.at[1, A_ROWS, :])
-    await_to("ag2-", cn.at[1, B_ROWS, :])
-    ffn(0, 2)
-    send("rs1", pt.at[1], rb.at[1], y2)
+    loop(2, ffn)
+    send("rs1", pt.at[1], rb.at[1], y2, lambda: rb.at[1])
     await_to("rs2", rb.at[3])
     await_to("rs3", rb.at[2])
 
@@ -691,8 +689,8 @@
     loop(4, add_far)
     for r in range(9):
         out[r] = acc[12 * r : 12 * r + 12, :].astype(BF)
-    for cp in sends.values():
-        cp.wait_send()
+    for name, like in sends.items():
+        remote(name, like(), like(), yp).wait_send()
     store_mid.wait()
 
 

time: 135 us -> 131 us (0.970)
  Pallas kernels: 131 us -> 127 us
    pallas_call x1, Pallas kernels: 131 us -> 127 us  [per_device(): pl.pallas_call(kernel, name='whole', out_shape=(jax.ShapeDtypeStruct((CEL...]
where the time goes in v5:
time: 131 us
  Pallas kernels  127 us (97%)
  local copies, waits for them, and re-layouts  3.02 us (2%)
    pallas_call x1, Pallas kernels, per_device(): pl.pallas_call(kernel, name='whole', out_shape=(jax.ShapeDtypeStruct((CEL...  127 us
    unnamed x4, local copies, waits for them, and re-layouts  3.02 us

profile of v5, /device:TPU:1, one launch (start us, length us, event | category | flops | bytes accessed | tf_op | source)
XLA Modules:
  0.0 130.6 jit_solution(10444250068131351393)
XLA Ops:
  0.6 127.0 %whole.1 = (bf16[432,1024]{1,0:T(8,128)(2,1)}, bf16[9,12,2048]{2,1,0:T(8,128)(2,1)}) custom-call(bf16[432,1024]{1,0:T(8,128)(2,1)} %bitcast.3, bf16[384,432]{1,0:T(8,128)(2,1)} %constant.13.clone.ps_in, bf16[576,432]{1,0:T(8,128)(2,1)} %constant.10.clone.p1_in, f32[3,16,128]{2,1,0:T(8,128)} %constant.14.clone.bias, bf16[1024,3072]{1,0:T(8,128)(2,1)} %qkvw.1, ...), custom_call_target="tpu_custom_call" | custom-call | tf_op jit(solution)/shard_map/whole/pallas_call | solution.py:711
  127.6 0.0 copy-start
  127.6 2.2 %copy.15 = bf16[18,24,1024]{2,1,0:T(8,128)(2,1)} copy(bf16[18,24,1024]{2,1,0:T(8,128)(2,1)} %bitcast.2) | data formatting | bytes 1769472
  129.8 0.0 copy-done
  129.8 0.8 copy.16
Async XLA Ops:
  127.6 2.2 %copy-start = (bf16[9,12,2048]{2,1,0:T(8,128)(2,1)S(1)}, bf16[9,12,2048]{2,1,0:T(8,128)(2,1)}, u32[]{:S(2)}) copy-start(bf16[9,12,2048]{2,1,0:T(8,128)(2,1)} %get-tuple-element.9) | copy-start | bytes 1327108

commit v6 on v5

--- a/solution.py
+++ b/solution.py
@@ -137,17 +137,20 @@
 
 HALO_SENDS = 8
 ORDER = (
-    ("x00", 3), ("ya+0", 3), ("ya-1", 3), ("ya+1", 7), ("ya-0", 7), ("z00a", 8), ("yb+", 11), ("yb-", 11),
-    ("n00", 11), ("x01", 12), ("yq+", 14), ("yq-", 14), ("x10", 15), ("z00b", 16), ("n01", 17), ("z01a", 17),
-    ("x11", 18), ("ye+", 20), ("ye-", 20), ("n10", 20), ("z10a", 20), ("x20", 21), ("z01b", 22), ("yt+", 23),
-    ("yt-", 23), ("n11", 23), ("x21", 24), ("z10b", 25), ("z11a", 25), ("n20", 26), ("x30", 27), ("z11b", 28),
-    ("z20a", 28), ("yu+", 29), ("yu-", 29), ("n21", 29), ("x31", 30), ("z20b", 31), ("z21a", 31), ("yef+", 32),
-    ("yef-", 32), ("n30", 32), ("x40", 33), ("z21b", 34), ("z30a", 34), ("yqf+", 35), ("yqf-", 35), ("n31", 35),
-    ("x41", 36), ("z30b", 37), ("z31a", 37), ("n40", 38), ("x50", 39), ("z31b", 40), ("z40a", 40), ("n41", 41),
-    ("x51", 42), ("z40b", 43), ("z41a", 43), ("n50", 44), ("x60", 46), ("z41b", 46), ("z50a", 46), ("n51", 48),
-    ("x61", 49), ("z50b", 50), ("z51a", 50), ("n60", 51), ("x70", 52), ("z51b", 53), ("z60a", 53), ("n61", 54),
-    ("x71", 55), ("z60b", 56), ("z61a", 56), ("n70", 57), ("z61b", 59), ("z70a", 59), ("n71", 60), ("z70b", 62),
-    ("z71a", 62), ("z71b", 65),
+    ("x00", 3), ("ya+0", 3), ("ya-1", 3), ("ya+1", 7), ("ya-0", 7), ("z00a", 8),
+    ("yb+", 11), ("yb-", 11), ("n00", 11), ("x01", 12), ("yq+", 14), ("yq-", 14),
+    ("x10", 15), ("z00b", 16), ("n01", 17), ("z01a", 17), ("x11", 18), ("ye+", 20),
+    ("ye-", 20), ("n10", 20), ("z10a", 20), ("x20", 21), ("z01b", 22), ("yt+", 23),
+    ("yt-", 23), ("n11", 23), ("x21", 24), ("z10b", 25), ("z11a", 25), ("n20", 26),
+    ("x30", 27), ("z11b", 28), ("z20a", 28), ("yu+", 29), ("yu-", 29), ("n21", 29),
+    ("x31", 30), ("z20b", 31), ("z21a", 31), ("yef+", 32), ("yef-", 32), ("n30", 32),
+    ("x40", 33), ("z21b", 34), ("z30a", 34), ("yqf+", 35), ("yqf-", 35), ("n31", 35),
+    ("x41", 36), ("z30b", 37), ("z31a", 37), ("n40", 38), ("x50", 39), ("z31b", 40),
+    ("z40a", 40), ("n41", 41), ("x51", 42), ("z40b", 43), ("z41a", 43), ("n50", 44),
+    ("x60", 46), ("z41b", 46), ("z50a", 46), ("n51", 48), ("x61", 49), ("z50b", 50),
+    ("z51a", 50), ("n60", 51), ("x70", 52), ("z51b", 53), ("z60a", 53), ("n61", 54),
+    ("x71", 55), ("z60b", 56), ("z61a", 56), ("n70", 57), ("z61b", 59), ("z70a", 59),
+    ("n71", 60), ("z70b", 62), ("z71a", 62), ("z71b", 65),
 )
 WSEMS = {}
 for _n in (
@@ -516,6 +519,7 @@
         kvh[:, cols(i, 256)] = jnp.dot(
             halo[...], qkvv[:, cols(i, 256, D)], preferred_element_type=F32
         ).astype(BF)
+        pump_at(i, {3: 21})
 
     pump(20)
     loop(8, project_halo)
@@ -534,6 +538,7 @@
         attr[:, cols(i, 256)] = jnp.dot(
             p1t[...], att[:, cols(i, 256)], preferred_element_type=F32
         ).astype(BF)
+        pump_at(i, {1: 37})
 
     loop(4, unpermute)
     local[4].wait()
@@ -541,6 +546,7 @@
     def out_project(i):
         mixed = jnp.dot(attr[...], outv[:, cols(i, 256)], preferred_element_type=F32)
         mid[:, cols(i, 256)] = (tok[:, cols(i, 256)].astype(F32) + mixed).astype(BF)
+        pump_at(i, {1: 38})
 
     loop(4, out_project)
     store_mid = pltpu.make_async_copy(mid, mid_out, lsem.at[9])
@@ -554,6 +560,7 @@
             pg[pl.ds(pl.multiple_of(g * GROUP, 16), GROUP), :], mid[:, cols(t, 256)],
             preferred_element_type=F32,
         ).astype(BF)
+        pump_at(i, {3: 39, 7: 40, 11: 41})
 
     loop(16, patch)
 
@@ -621,9 +628,7 @@
 
     send("ag+", cn.at[0], cn.at[2], yp, lambda: cn.at[2])
     send("ag-", cn.at[0], cn.at[3], ym, lambda: cn.at[3])
-    pump(57)
-    need_far(4)
-    share(4)
+    pump(58)
     for n in (7, 8):
         local[n].wait()
     await_to("up", up4.at[1])
@@ -663,6 +668,9 @@
     send("ag2+", cn.at[2, A_ROWS, :], cn.at[1, A_ROWS, :], yp, lambda: cn.at[1, A_ROWS, :])
     await_to("ag-", cn.at[3])
     send("ag2-", cn.at[3, B_ROWS, :], cn.at[1, B_ROWS, :], ym, lambda: cn.at[1, B_ROWS, :])
+    pump(60)
+    need_far(4)
+    share(4)
     pump(99)
     for k in (5, 6, 7):
         need_far(k)

time: 131 us -> 126 us (0.962)
  Pallas kernels: 127 us -> 122 us
    pallas_call x1, Pallas kernels: 127 us -> 122 us  [per_device(): pl.pallas_call(kernel, name='whole', out_shape=(jax.ShapeDtypeStruct((CEL...]
where the time goes in v6:
time: 126 us
  Pallas kernels  122 us (97%)
  local copies, waits for them, and re-layouts  3.02 us (2%)
    pallas_call x1, Pallas kernels, per_device(): pl.pallas_call(kernel, name='whole', out_shape=(jax.ShapeDtypeStruct((CEL...  122 us
    unnamed x4, local copies, waits for them, and re-layouts  3.02 us

profile of v6, /device:TPU:1, one launch (start us, length us, event | category | flops | bytes accessed | tf_op | source)
XLA Modules:
  0.0 126.0 jit_solution(9745889402474624522)
XLA Ops:
  0.6 122.4 %whole.1 = (bf16[432,1024]{1,0:T(8,128)(2,1)}, bf16[9,12,2048]{2,1,0:T(8,128)(2,1)}) custom-call(bf16[432,1024]{1,0:T(8,128)(2,1)} %bitcast.3, bf16[384,432]{1,0:T(8,128)(2,1)} %constant.13.clone.ps_in, bf16[576,432]{1,0:T(8,128)(2,1)} %constant.10.clone.p1_in, f32[3,16,128]{2,1,0:T(8,128)} %constant.14.clone.bias, bf16[1024,3072]{1,0:T(8,128)(2,1)} %qkvw.1, ...), custom_call_target="tpu_custom_call" | custom-call | tf_op jit(solution)/shard_map/whole/pallas_call | solution.py:719
  123.0 0.0 copy-start
  123.0 2.2 %copy.15 = bf16[18,24,1024]{2,1,0:T(8,128)(2,1)} copy(bf16[18,24,1024]{2,1,0:T(8,128)(2,1)} %bitcast.2) | data formatting | bytes 1769472
  125.2 0.0 copy-done
  125.2 0.8 copy.16
Async XLA Ops:
  123.0 2.2 %copy-start = (bf16[9,12,2048]{2,1,0:T(8,128)(2,1)S(1)}, bf16[9,12,2048]{2,1,0:T(8,128)(2,1)}, u32[]{:S(2)}) copy-start(bf16[9,12,2048]{2,1,0:T(8,128)(2,1)} %get-tuple-element.9) | copy-start | bytes 1327108

commit v7 on v6

--- a/solution.py
+++ b/solution.py
@@ -634,6 +634,10 @@
     await_to("up", up4.at[1])
     await_to("down", down4.at[1])
 
+    def await_share(k):
+        size = 1024 if k < 6 else 256
+        await_to(f"s{k}", (up4 if k < 6 else down4).at[3, pl.ds((k % 2) * size, size), :])
+
     def ffn(n):
         first = 2 - 2 * n
         rows = 2 * GROUP
@@ -645,6 +649,13 @@
             hid[:, cols(i, 256)] = gelu(h).astype(BF)
 
         loop(8, up_step)
+
+        @pl.when(n == 0)
+        def _():
+            need_far(7)
+            share(7)
+            await_share(6)
+            await_share(7)
 
         def down_step(i):
             t = cols(i, 256)
@@ -672,12 +683,11 @@
     need_far(4)
     share(4)
     pump(99)
-    for k in (5, 6, 7):
+    for k in (5, 6):
         need_far(k)
         share(k)
-    for k in (4, 5, 6, 7):
-        size = 1024 if k < 6 else 256
-        await_to(f"s{k}", (up4 if k < 6 else down4).at[3, pl.ds((k % 2) * size, size), :])
+    for k in (4, 5):
+        await_share(k)
     loop(2, ffn)
     send("rs1", pt.at[1], rb.at[1], y2, lambda: rb.at[1])
     await_to("rs2", rb.at[3])

time: 126 us -> 124 us (0.984)
  Pallas kernels: 122 us -> 120 us
    pallas_call x1, Pallas kernels: 122 us -> 120 us  [per_device(): pl.pallas_call(kernel, name='whole', out_shape=(jax.ShapeDtypeStruct((CEL...]
where the time goes in v7:
time: 124 us; the launch traced here: 123 us
  Pallas kernels  120 us (97%)
  local copies, waits for them, and re-layouts  3.02 us (2%)
    pallas_call x1, Pallas kernels, per_device(): pl.pallas_call(kernel, name='whole', out_shape=(jax.ShapeDtypeStruct((CEL...  120 us
    unnamed x4, local copies, waits for them, and re-layouts  3.02 us

profile of v7, /device:TPU:1, one launch (start us, length us, event | category | flops | bytes accessed | tf_op | source)
XLA Modules:
  0.0 123.3 jit_solution(6872804542500041198)
XLA Ops:
  0.6 119.6 %whole.1 = (bf16[432,1024]{1,0:T(8,128)(2,1)}, bf16[9,12,2048]{2,1,0:T(8,128)(2,1)}) custom-call(bf16[432,1024]{1,0:T(8,128)(2,1)} %bitcast.3, bf16[384,432]{1,0:T(8,128)(2,1)} %constant.13.clone.ps_in, bf16[576,432]{1,0:T(8,128)(2,1)} %constant.10.clone.p1_in, f32[3,16,128]{2,1,0:T(8,128)} %constant.14.clone.bias, bf16[1024,3072]{1,0:T(8,128)(2,1)} %qkvw.1, ...), custom_call_target="tpu_custom_call" | custom-call | tf_op jit(solution)/shard_map/whole/pallas_call | solution.py:729
  120.3 0.0 copy-start
  120.3 2.2 %copy.15 = bf16[18,24,1024]{2,1,0:T(8,128)(2,1)} copy(bf16[18,24,1024]{2,1,0:T(8,128)(2,1)} %bitcast.2) | data formatting | bytes 1769472
  122.5 0.0 copy-done
  122.5 0.8 copy.16
Async XLA Ops:
  120.3 2.2 %copy-start = (bf16[9,12,2048]{2,1,0:T(8,128)(2,1)S(1)}, bf16[9,12,2048]{2,1,0:T(8,128)(2,1)}, u32[]{:S(2)}) copy-start(bf16[9,12,2048]{2,1,0:T(8,128)(2,1)} %get-tuple-element.9) | copy-start | bytes 1327108

commit v8 on v7

--- a/solution.py
+++ b/solution.py
@@ -682,10 +682,12 @@
     pump(60)
     need_far(4)
     share(4)
+    pump(63)
+    need_far(5)
+    share(5)
     pump(99)
-    for k in (5, 6):
-        need_far(k)
-        share(k)
+    need_far(6)
+    share(6)
     for k in (4, 5):
         await_share(k)
     loop(2, ffn)

time: 124 us -> 123 us (level)
  no operation moved by 1% of the time
where the time goes in v8:
time: 123 us
  Pallas kernels  119 us (97%)
  local copies, waits for them, and re-layouts  3.02 us (2%)
    pallas_call x1, Pallas kernels, per_device(): pl.pallas_call(kernel, name='whole', out_shape=(jax.ShapeDtypeStruct((CEL...  119 us
    unnamed x4, local copies, waits for them, and re-layouts  3.02 us

profile of v8, /device:TPU:1, one launch (start us, length us, event | category | flops | bytes accessed | tf_op | source)
XLA Modules:
  0.0 122.6 jit_solution(2155151819816802410)
XLA Ops:
  0.6 118.9 %whole.1 = (bf16[432,1024]{1,0:T(8,128)(2,1)}, bf16[9,12,2048]{2,1,0:T(8,128)(2,1)}) custom-call(bf16[432,1024]{1,0:T(8,128)(2,1)} %bitcast.3, bf16[384,432]{1,0:T(8,128)(2,1)} %constant.13.clone.ps_in, bf16[576,432]{1,0:T(8,128)(2,1)} %constant.10.clone.p1_in, f32[3,16,128]{2,1,0:T(8,128)} %constant.14.clone.bias, bf16[1024,3072]{1,0:T(8,128)(2,1)} %qkvw.1, ...), custom_call_target="tpu_custom_call" | custom-call | tf_op jit(solution)/shard_map/whole/pallas_call | solution.py:731
  119.6 0.0 copy-start
  119.6 2.2 %copy.15 = bf16[18,24,1024]{2,1,0:T(8,128)(2,1)} copy(bf16[18,24,1024]{2,1,0:T(8,128)(2,1)} %bitcast.2) | data formatting | bytes 1769472
  121.8 0.0 copy-done
  121.8 0.8 copy.16
Async XLA Ops:
  119.6 2.2 %copy-start = (bf16[9,12,2048]{2,1,0:T(8,128)(2,1)S(1)}, bf16[9,12,2048]{2,1,0:T(8,128)(2,1)}, u32[]{:S(2)}) copy-start(bf16[9,12,2048]{2,1,0:T(8,128)(2,1)} %get-tuple-element.9) | copy-start | bytes 1327108
